TPU v7x, 128 devices: a whole 4x4x4 slice. The times are simulated.
128 devices in a mesh: batch: 16 (over y, x), proto: 8 (over z, core).
Axes of the slice: x: 4, y: 4, z: 4, core: 2. Of those that a mesh axis runs over, the one named last changes fastest.
Arguments:
- teacher_emb: bfloat16 [16384, 256], P('batch'), may hold values from -24 to 24
- student_emb: bfloat16 [16384, 256], P('batch'), may hold values from -24 to 24
- prototypes: bfloat16 [256, 65536], P(None, 'proto'), may hold values from -2 to 2
Outputs:
- crop_loss: float32 [16384], P('batch')
- proto_grad: float32 [256, 65536], P('batch', 'proto')
All inputs are finite; a program needn't handle non-finite values.
Results may differ from a plain program's by a relative error of at most 0.0085.
Values sent between devices are 32-bit elements; how exact they have to be, the bound alone decides.
A program may use at most 192 MiB of HBM per device.

v0:
```python
import math

import jax
import jax.numpy as jnp
from jax import lax
from jax.sharding import PartitionSpec as P

PROTOS = 65536
ITERS = 3


TEACHER_TEMP = 0.07
STUDENT_TEMP = 0.1


def unit_rows(values, axis):
    wide = values.astype(jnp.float32)
    return (wide * lax.rsqrt(jnp.sum(wide * wide, axis=axis, keepdims=True) + 1e-06)).astype(
        jnp.bfloat16
    )


def local(teacher_emb, student_emb, prototypes):
    crop_count = teacher_emb.shape[0] * lax.axis_size("batch")
    unit_teacher = unit_rows(teacher_emb, 1)
    unit_student = unit_rows(student_emb, 1)
    unit_protos = unit_rows(prototypes, 0)
    teacher = jnp.dot(unit_teacher, unit_protos, preferred_element_type=jnp.float32) / TEACHER_TEMP
    offset = jnp.zeros((teacher_emb.shape[0],), jnp.float32)
    proto_shift = jnp.zeros((prototypes.shape[1],), jnp.float32)
    for sweep_index in range(ITERS):
        col_local = jnp.sum(jnp.exp(teacher + offset[:, None]), axis=0)
        proto_shift = -math.log(PROTOS) - jnp.log(lax.psum(col_local, "batch"))
        row_local = jnp.sum(jnp.exp(teacher + proto_shift[None, :]), axis=1)
        row_total = lax.psum(row_local, "proto")
        offset = -math.log(crop_count) - jnp.log(row_total)
    target = jnp.exp(teacher + proto_shift[None, :] + offset[:, None] + math.log(crop_count))
    student = jnp.dot(unit_student, unit_protos, preferred_element_type=jnp.float32) / STUDENT_TEMP
    summed, cross = lax.psum(
        (jnp.sum(jnp.exp(student), axis=1), jnp.sum(target * student, axis=1)), "proto"
    )
    log_total = jnp.log(summed)
    crop_loss = log_total - cross
    student_prob = jnp.exp(student - log_total[:, None])
    factor = PROTOS / (STUDENT_TEMP * crop_count)
    grad_scaled = ((student_prob - target) * factor).astype(jnp.bfloat16)
    proto_grad = lax.psum_scatter(
        lax.dot_general(
            unit_student, grad_scaled, (((0,), (0,)), ((), ())), preferred_element_type=jnp.float32
        ),
        "batch",
        scatter_dimension=0,
        tiled=True,
    )
    return (crop_loss, proto_grad)


def solution(mesh):
    in_specs = (P("batch", None), P("batch", None), P(None, "proto"))
    out_specs = (P("batch"), P("batch", "proto"))
    return jax.shard_map(local, mesh=mesh, in_specs=in_specs, out_specs=out_specs, check_vma=False)
```

profile of v0, /device:TPU:0, one launch (start us, length us, event | category | flops | bytes accessed | tf_op | source)
XLA Modules:
  0.0 506.7 jit_solution(3921874890823429547)
XLA Ops:
  7.2 0.0 reduce-scatter.2.cloned.1.call-start
  7.2 1.3 fusion.9
  8.5 1.3 fusion.7
  9.8 3.1 fusion.1
  12.8 15.4 %exponential_reduce_fusion.5 = (f32[8192]{0:T(1024)S(1)}, f32[1024,8192]{1,0:T(8,128)}) fusion(bf16[256,8192]{1,0:T(8,128)(2,1)} %param.5, f32[8192]{0:T(1024)S(1)} %add_rsqrt_fusion, bf16[1024,256]{1,0:T(8,128)(2,1)} %param.3, f32[1024]{0:T(1024)S(1)} %add_rsqrt_fusion.1), kind=kOutput, calls=%fused_computation.8 | convolution fusion | flops 4318814208 | bytes 38342656 | tf_op jit(solution)/shard_map/dot_general | solution.py:28
  28.2 74.7 %psum.57 = f32[8192]{0:T(1024)S(1)} all-reduce(f32[8192]{0:T(1024)S(1)} %get-tuple-element.8), channel_id=1, replica_groups=mesh['batch'=16,'proto'=8] {'batch'}, use_global_device_ids=true, to_apply=%region_6.0 | all-reduce | flops 8192 | bytes 65536 | tf_op jit(solution)/shard_map/psum | solution.py:33
  102.9 13.8 %exponential_reduce_fusion.4 = f32[1024]{0:T(1024)S(1)} fusion(f32[1024,8192]{1,0:T(8,128)} %get-tuple-element.9, f32[8192]{0:T(1024)S(1)} %log_subtract_fusion.2), kind=kLoop, calls=%fused_computation.7 | loop fusion | flops 25164800 | bytes 33591296 | tf_op jit(solution)/shard_map/reduce_sum | solution.py:34
  116.7 13.1 %psum.58 = f32[1024]{0:T(1024)S(1)} all-reduce(f32[1024]{0:T(1024)S(1)} %exponential_reduce_fusion.4), channel_id=1, replica_groups=mesh['batch'=16,'proto'=8] {'proto'}, use_global_device_ids=true, to_apply=%region_8.0 | all-reduce | flops 1024 | bytes 8192 | tf_op jit(solution)/shard_map/psum | solution.py:35
  129.8 14.0 %exponential_reduce_fusion.3 = f32[8192]{0:T(1024)S(1)} fusion(f32[1024,8192]{1,0:T(8,128)} %get-tuple-element.9, f32[1024]{0:T(1024)S(1)} %log_subtract_fusion.5), kind=kLoop, calls=%fused_computation.6 | loop fusion | flops 25157632 | bytes 33591296 | tf_op jit(solution)/shard_map/reduce_sum | solution.py:32
  143.8 69.5 %psum.59 = f32[8192]{0:T(1024)S(1)} all-reduce(f32[8192]{0:T(1024)S(1)} %exponential_reduce_fusion.3), channel_id=1, replica_groups=mesh['batch'=16,'proto'=8] {'batch'}, use_global_device_ids=true, to_apply=%region_10.0 | all-reduce | flops 8192 | bytes 65536 | tf_op jit(solution)/shard_map/psum | solution.py:33
  213.4 13.8 %exponential_reduce_fusion.2 = f32[1024]{0:T(1024)S(1)} fusion(f32[1024,8192]{1,0:T(8,128)} %get-tuple-element.9, f32[8192]{0:T(1024)S(1)} %log_subtract_fusion.1), kind=kLoop, calls=%fused_computation.5 | loop fusion | flops 25164800 | bytes 33591296 | tf_op jit(solution)/shard_map/reduce_sum | solution.py:34
  227.2 12.4 %psum.60 = f32[1024]{0:T(1024)S(1)} all-reduce(f32[1024]{0:T(1024)S(1)} %exponential_reduce_fusion.2), channel_id=1, replica_groups=mesh['batch'=16,'proto'=8] {'proto'}, use_global_device_ids=true, to_apply=%region_12.0 | all-reduce | flops 1024 | bytes 8192 | tf_op jit(solution)/shard_map/psum | solution.py:35
  239.6 0.0 copy-start
  239.6 14.0 %exponential_reduce_fusion.1 = f32[8192]{0:T(1024)S(1)} fusion(f32[1024,8192]{1,0:T(8,128)} %get-tuple-element.9, f32[1024]{0:T(1024)S(1)} %log_subtract_fusion.4), kind=kLoop, calls=%fused_computation.4 | loop fusion | flops 25157632 | bytes 33591296 | tf_op jit(solution)/shard_map/reduce_sum | solution.py:32
  253.7 69.5 %psum.61 = f32[8192]{0:T(1024)S(1)} all-reduce(f32[8192]{0:T(1024)S(1)} %exponential_reduce_fusion.1), channel_id=1, replica_groups=mesh['batch'=16,'proto'=8] {'batch'}, use_global_device_ids=true, to_apply=%region_14.0 | all-reduce | flops 8192 | bytes 65536 | tf_op jit(solution)/shard_map/psum | solution.py:33
  323.2 13.8 %exponential_reduce_fusion = f32[1024]{0:T(1024)S(1)} fusion(f32[1024,8192]{1,0:T(8,128)} %get-tuple-element.9, f32[8192]{0:T(1024)S(1)} %log_subtract_fusion), kind=kLoop, calls=%fused_computation.3 | loop fusion | flops 25164800 | bytes 33591296 | tf_op jit(solution)/shard_map/reduce_sum | solution.py:34
  337.0 12.6 %psum.62 = f32[1024]{0:T(1024)S(1)} all-reduce(f32[1024]{0:T(1024)S(1)} %exponential_reduce_fusion), channel_id=1, replica_groups=mesh['batch'=16,'proto'=8] {'proto'}, use_global_device_ids=true, to_apply=%region_16.0 | all-reduce | flops 1024 | bytes 8192 | tf_op jit(solution)/shard_map/psum | solution.py:35
  349.6 0.0 copy-done
  349.7 29.7 %exponential_reduce_fusion.6 = (f32[1024]{0:T(1024)S(1)}, f32[1024]{0:T(1024)S(1)}, f32[1024,8192]{1,0:T(8,128)}) fusion(f32[1024]{0:T(1024)S(1)} %log_subtract_fusion.3, f32[8192]{0:T(1024)S(1)} %log_subtract_fusion, f32[1024,8192]{1,0:T(8,128)} %get-tuple-element.9, bf16[256,8192]{1,0:T(8,128)(2,1)} %param.5, f32[8192]{0:T(1024)S(1)} %add_rsqrt_fusion, ...), kind=kOutput, calls=%fused_computation.9 | convolution fusion | flops 4369152000 | bytes 71909376 | tf_op jit(solution)/shard_map/dot_general | solution.py:38
  379.4 12.6 %all-reduce = (f32[1024]{0:T(1024)S(1)}, f32[1024]{0:T(1024)S(1)}) all-reduce(f32[1024]{0:T(1024)S(1)} %get-tuple-element.3, f32[1024]{0:T(1024)S(1)} %get-tuple-element.2), channel_id=1, replica_groups=mesh['batch'=16,'proto'=8] {'proto'}, use_global_device_ids=true, to_apply=%region_18.0 | all-reduce | flops 2048 | bytes 16384 | tf_op jit(solution)/shard_map/psum | solution.py:39
  392.1 0.6 fusion.19
  392.7 28.7 %fusion = f32[256,8192]{1,0:T(8,128)} fusion(f32[1024,8192]{1,0:T(8,128)} %get-tuple-element.10, f32[1024,8192]{1,0:T(8,128)} %get-tuple-element.9, f32[1024]{0:T(1024)S(1)} %get-tuple-element.6, f32[1024]{0:T(1024)S(1)} %log_subtract_fusion.3, f32[8192]{0:T(1024)S(1)} %log_subtract_fusion, bf16[1024,256]{1,0:T(8,128)(2,1)S(1)} %copy-done, ...), kind=kOutput, calls=%fused_computation.10 | convolution fusion | flops 4371251200 | bytes 76066816 | tf_op jit(solution)/shard_map/dot_general | solution.py:48
  421.3 0.0 reduce-scatter.2.cloned.1.call-update
  421.4 78.5 %reduce-scatter.2.cloned.1.call-done = f32[16,8192]{1,0:T(8,128)} async-done(((f32[256,8192]{1,0:T(8,128)}), f32[16,8192]{1,0:T(8,128)}) %reduce-scatter.2.cloned.1.call-update) | async-done | bytes 524304 | tf_op jit(solution)/shard_map/reduce_scatter | solution.py:47
  (9 shorter events, 0.1 us)
Async XLA Ops:
  7.2 492.7 %reduce-scatter.2.cloned.1.call-start = ((), (), s32[]{:S(2)}) async-start(), calls=%async_computation.1 | async-start | bytes 8912896 | tf_op jit(solution)/shard_map/reduce_scatter | solution.py:47
  239.6 110.0 %copy-start = (bf16[1024,256]{1,0:T(8,128)(2,1)S(1)}, bf16[1024,256]{1,0:T(8,128)(2,1)}, u32[]{:S(2)}) copy-start(bf16[1024,256]{1,0:T(8,128)(2,1)} %param.4) | copy-start | bytes 1572868
Sparse Core Ops, SparseCore 0:
  421.5 78.3 reduce-scatter.1
where the time goes:
time: 508 us; the launch traced here: 507 us
  blocking collectives  265 us (52%)
  waiting for transfers between devices  78.5 us (15%)
  other arithmetic  75.6 us (15%)
  matrix products  73.8 us (15%)
  between operations  14.1 us (3%)
    psum x3, blocking collectives, local(): proto_shift = -math.log(PROTOS) - jnp.log(lax.psum(col_local, 'batch'))  214 us
    reduce_scatter x1, waiting for transfers between devices, local(): lax.psum_scatter(lax.dot_general(unit_student, grad_scaled, (((0,), (0,))...  78.5 us
    reduce_sum x3, other arithmetic, local(): row_local = jnp.sum(jnp.exp(teacher + proto_shift[None, :]), axis=1)  41.4 us
    psum x3, blocking collectives, local(): row_total = lax.psum(row_local, 'proto')  38.2 us
    dot_general x1, matrix products, local(): jnp.dot(unit_student, unit_protos, preferred_element_type=jnp.float32)  29.7 us
    dot_general x1, matrix products, local(): lax.dot_general(unit_student, grad_scaled, (((0,), (0,)), ((), ())), pref...  28.7 us
    reduce_sum x2, other arithmetic, local(): col_local = jnp.sum(jnp.exp(teacher + offset[:, None]), axis=0)  28 us
    dot_general x1, matrix products, local(): jnp.dot(unit_teacher, unit_protos, preferred_element_type=jnp.float32)  15.4 us
  transfers between devices with their start and end apart: 1, of which 1 were waited for; matrix products, arithmetic and copies ran while one was open for 0% of the time, Pallas kernels for 0%

commit v1 on v0

v1 whole, which is shorter than its diff:
```python
import functools
import math

import jax
import jax.numpy as jnp
from jax import lax
from jax.experimental import pallas as pl
from jax.experimental.pallas import tpu as pltpu
from jax.sharding import PartitionSpec as P

PROTOS = 65536
CROPS = 16384
ITERS = 3
TEACHER_TEMP = 0.07
STUDENT_TEMP = 0.1
NB = 16
NP = 8
ROWS = 1024
COLS = 8192
D = 256
LOG2E = 1.4426950408889634
MESH = pl.DeviceIdType.MESH
F32 = jnp.float32
BF16 = jnp.bfloat16


def unit(values, axis):
    wide = values.astype(F32)
    return (wide * lax.rsqrt(jnp.sum(wide * wide, axis=axis, keepdims=True) + 1e-06)).astype(BF16)


def rows_to_vec(part):
    out = []
    for i in range(8):
        block = part[pl.ds(i * 128, 128), :]
        out.append(jnp.sum(block.T, axis=0, keepdims=True))
    return jnp.concatenate(out, axis=0)


def vec_to_rows(vec, out):
    for i in range(8):
        out[pl.ds(i * 128, 128), :] = jnp.broadcast_to(vec[i : i + 1, :], (128, 128)).T


def kernel(
    te, se, pr, loss, grad,
    ut, us, ust, up, big, part, wide, col, col_in, cvec, rvec, row_in, gbuf, zvec, z_in, xvec, x_in,
    s_col, r_col, s_c, r_c, s_row, r_row,
):
    mb = lax.axis_index("batch")
    mp = lax.axis_index("proto")
    barrier = pltpu.get_barrier_semaphore()

    def greet_batch(d, carry):
        pl.semaphore_signal(barrier, inc=1, device_id={"batch": lax.rem(mb + d, NB)}, device_id_type=MESH)
        return carry

    def greet_proto(d, carry):
        pl.semaphore_signal(barrier, inc=1, device_id={"proto": lax.rem(mp + d, NP)}, device_id_type=MESH)
        return carry

    lax.fori_loop(1, NB, greet_batch, 0)
    lax.fori_loop(1, NP, greet_proto, 0)

    ut[...] = unit(te[...], 1)
    us[...] = unit(se[...], 1)
    for i in range(8):
        block = us[pl.ds(i * 128, 128), :]
        ust[:, pl.ds(i * 128, 128)] = block.astype(F32).T.astype(BF16)

    def first(j, carry):
        cols = pl.ds(pl.multiple_of(j * 512, 512), 512)
        w = unit(pr[:, cols], 0)
        up[:, cols] = w
        total = jnp.zeros((8, 512), F32)
        for i in range(4):
            rows = pl.ds(i * 256, 256)
            e = jnp.exp2(jnp.dot(ut[rows, :], w, preferred_element_type=F32) * (LOG2E / TEACHER_TEMP))
            big[rows, cols] = e
            total = total + jnp.sum(e.reshape(32, 8, 512), axis=0)
        flat = jnp.sum(total, axis=0, keepdims=True)
        for k in range(4):
            col[0, j, pl.ds(k, 1), :] = flat[:, k * 128 : (k + 1) * 128]
        return carry

    lax.fori_loop(0, 16, first, 0)
    pl.semaphore_wait(barrier, NB + NP - 2)

    def sum_cols(it):
        def send(d, carry):
            to = lax.rem(mb + d, NB)
            pltpu.make_async_remote_copy(
                src_ref=col.at[it, to], dst_ref=col_in.at[it, mb],
                send_sem=s_col.at[it], recv_sem=r_col.at[it],
                device_id={"batch": to}, device_id_type=MESH,
            ).start()
            return carry

        lax.fori_loop(1, NB, send, 0)
        col_in[it, mb] = col[it, mb]
        some = col_in.at[it, pl.ds(0, NB - 1)]
        pltpu.make_async_copy(some, some, r_col.at[it]).wait()
        total = jnp.sum(col_in[it], axis=0)
        cvec[it, mb] = 1.0 / (total * PROTOS)

        def spread(d, carry):
            to = lax.rem(mb + d, NB)
            pltpu.make_async_remote_copy(
                src_ref=cvec.at[it, mb], dst_ref=cvec.at[it, mb],
                send_sem=s_c.at[it], recv_sem=r_c.at[it],
                device_id={"batch": to}, device_id_type=MESH,
            ).start()
            return carry

        lax.fori_loop(1, NB, spread, 0)
        some = cvec.at[it, pl.ds(0, NB - 1)]
        pltpu.make_async_copy(some, some, r_c.at[it]).wait()

    def send_rows(src, dst, k):
        def send(d, carry):
            to = lax.rem(mp + d, NP)
            pltpu.make_async_remote_copy(
                src_ref=src, dst_ref=dst.at[mp],
                send_sem=s_row.at[k], recv_sem=r_row.at[k],
                device_id={"proto": to}, device_id_type=MESH,
            ).start()
            return carry

        lax.fori_loop(1, NP, send, 0)

    def wait_rows(src, dst, k):
        dst[mp] = src[...]
        some = dst.at[pl.ds(0, NP - 1)]
        pltpu.make_async_copy(some, some, r_row.at[k]).wait()
        return jnp.sum(dst[...], axis=0)

    def row_pass(it):
        def step(r, carry):
            rows = pl.ds(pl.multiple_of(r * 64, 64), 64)
            acc = jnp.zeros((64, 128), F32)
            for j in range(64):
                acc = acc + big[rows, pl.ds(j * 128, 128)] * cvec[it, j // 4, pl.ds(j % 4, 1), :]
            part[rows, :] = acc
            return carry

        lax.fori_loop(0, 16, step, 0)

    def col_pass(it):
        for g in range(4):
            def step(i, acc):
                acc = list(acc)
                for u in range(4):
                    rows = pl.ds(pl.multiple_of(i * 32 + u * 8, 8), 8)
                    a = wide[rows, :]
                    for k in range(16):
                        acc[k] = acc[k] + big[rows, pl.ds(g * 2048 + k * 128, 128)] * a
                return tuple(acc)

            acc = lax.fori_loop(0, 32, step, tuple(jnp.zeros((8, 128), F32) for _ in range(16)))
            for k in range(16):
                j = g * 16 + k
                col[it, j // 4, pl.ds(j % 4, 1), :] = jnp.sum(acc[k], axis=0, keepdims=True)

    for it in range(ITERS):
        if it:
            col_pass(it)
        sum_cols(it)
        row_pass(it)
        rvec[it] = rows_to_vec(part)
        send_rows(rvec.at[it], row_in.at[it], it)
        if it == 0:
            def student(r, carry):
                rows = pl.ds(pl.multiple_of(r * 256, 256), 256)
                acc = jnp.zeros((256, 128), F32)
                for j in range(16):
                    s = jnp.dot(us[rows, :], up[:, pl.ds(j * 512, 512)], preferred_element_type=F32)
                    e = jnp.exp2(s * (LOG2E / STUDENT_TEMP))
                    for k in range(4):
                        acc = acc + e[:, k * 128 : (k + 1) * 128]
                part[rows, :] = acc
                return carry

            lax.fori_loop(0, 4, student, 0)
            zvec[...] = rows_to_vec(part)
            send_rows(zvec, z_in, 3)
        total = wait_rows(rvec.at[it], row_in.at[it], it)
        a = 1.0 / (total * CROPS)
        if it < ITERS - 1:
            vec_to_rows(a, wide)

    factor = PROTOS / (STUDENT_TEMP * CROPS)
    z = wait_rows(zvec, z_in, 3)
    vec_to_rows(a * CROPS, wide)
    vec_to_rows(1.0 / z, part)
    xpart = gbuf[1]

    def last(j, carry):
        cols = pl.ds(pl.multiple_of(j * 256, 256), 256)
        w = up[:, cols]
        c0 = cvec[ITERS - 1, j // 2, pl.ds((j % 2) * 2, 1), :]
        c1 = cvec[ITERS - 1, j // 2, pl.ds((j % 2) * 2 + 1, 1), :]
        c = jnp.concatenate([c0, c1], axis=1)
        for i in range(8):
            rows = pl.ds(i * 128, 128)
            s = jnp.dot(us[rows, :], w, preferred_element_type=F32)
            wa = wide[rows, :]
            pz = part[rows, :]
            t = big[rows, cols] * jnp.concatenate([wa, wa], axis=1) * c
            p = jnp.exp2(s * (LOG2E / STUDENT_TEMP)) * jnp.concatenate([pz, pz], axis=1)
            gbuf[0][rows, :] = ((p - t) * factor).astype(BF16)
            ts = t * s
            xpart[rows, :] += ts[:, :128] + ts[:, 128:]
        grad[:, cols] = jnp.dot(ust[...], gbuf[0][...], preferred_element_type=F32)
        return carry

    xpart[...] = jnp.zeros((ROWS, 128), F32)
    lax.fori_loop(0, 32, last, 0)
    xvec[...] = rows_to_vec(xpart) * (1.0 / STUDENT_TEMP)
    send_rows(xvec, x_in, 4)
    x = wait_rows(xvec, x_in, 4)
    loss[...] = jnp.log(z) - x

    for it in range(ITERS):
        some = col.at[it, pl.ds(0, NB - 1)]
        pltpu.make_async_copy(some, some, s_col.at[it]).wait()
        pltpu.make_async_copy(some, some, s_c.at[it]).wait()
    for k in range(5):
        some = z_in.at[pl.ds(0, NP - 1)]
        pltpu.make_async_copy(some, some, s_row.at[k]).wait()


def local(teacher_emb, student_emb, prototypes):
    vmem = pl.BlockSpec(memory_space=pltpu.VMEM)
    loss, grad = pl.pallas_call(
        kernel,
        out_shape=(
            jax.ShapeDtypeStruct((8, 128), F32),
            jax.ShapeDtypeStruct((D, COLS), F32),
        ),
        in_specs=[vmem] * 3,
        out_specs=(vmem, vmem),
        scratch_shapes=[
            pltpu.VMEM((ROWS, D), BF16),
            pltpu.VMEM((ROWS, D), BF16),
            pltpu.VMEM((D, ROWS), BF16),
            pltpu.VMEM((D, COLS), BF16),
            pltpu.VMEM((ROWS, COLS), F32),
            pltpu.VMEM((ROWS, 128), F32),
            pltpu.VMEM((ROWS, 128), F32),
            pltpu.VMEM((ITERS, NB, 4, 128), F32),
            pltpu.VMEM((ITERS, NB, 4, 128), F32),
            pltpu.VMEM((ITERS, NB, 4, 128), F32),
            pltpu.VMEM((ITERS, 8, 128), F32),
            pltpu.VMEM((ITERS, NP, 8, 128), F32),
            [pltpu.VMEM((ROWS, D), BF16), pltpu.VMEM((ROWS, 128), F32)],
            pltpu.VMEM((8, 128), F32),
            pltpu.VMEM((NP, 8, 128), F32),
            pltpu.VMEM((8, 128), F32),
            pltpu.VMEM((NP, 8, 128), F32),
            pltpu.SemaphoreType.DMA((ITERS,)),
            pltpu.SemaphoreType.DMA((ITERS,)),
            pltpu.SemaphoreType.DMA((ITERS,)),
            pltpu.SemaphoreType.DMA((ITERS,)),
            pltpu.SemaphoreType.DMA((5,)),
            pltpu.SemaphoreType.DMA((5,)),
        ],
        compiler_params=pltpu.CompilerParams(
            collective_id=0, has_side_effects=True, vmem_limit_bytes=62 * 1024 * 1024
        ),
    )(teacher_emb, student_emb, prototypes)
    grad = lax.psum_scatter(grad, "batch", scatter_dimension=0, tiled=True)
    return loss.reshape(ROWS), grad


def solution(mesh):
    in_specs = (P("batch", None), P("batch", None), P(None, "proto"))
    out_specs = (P("batch"), P("batch", "proto"))
    return jax.shard_map(local, mesh=mesh, in_specs=in_specs, out_specs=out_specs, check_vma=False)
```

time: 508 us -> 202 us (0.40)
  blocking collectives: 265 us -> 0 us
  Pallas kernels: 0 us -> 104 us
  other arithmetic: 75.6 us -> 0 us
  matrix products: 73.8 us -> 0 us
    psum x7 -> x0, blocking collectives: 265 us -> none  [the longest x3 214 us: local(): proto_shift = -math.log(PROTOS) - jnp.log(lax.psum(col_local, 'batch'))]
    pallas_call x0 -> x1, Pallas kernels: none -> 104 us  [local(): pl.pallas_call(kernel, out_shape=(jax.ShapeDtypeStruct((8, 128), F32), ja...]
    reduce_sum x8 -> x0, other arithmetic: 75 us -> none  [the longest x3 41.4 us: local(): row_local = jnp.sum(jnp.exp(teacher + proto_shift[None, :]), axis=1)]
    dot_general x3 -> x0, matrix products: 73.8 us -> none  [the longest x1 29.7 us: local(): jnp.dot(unit_student, unit_protos, preferred_element_type=jnp.float32)]
where the time goes in v1:
time: 202 us
  Pallas kernels  104 us (51%)
  waiting for transfers between devices  83.1 us (41%)
  between operations  14 us (7%)
    pallas_call x1, Pallas kernels, local(): pl.pallas_call(kernel, out_shape=(jax.ShapeDtypeStruct((8, 128), F32), ja...  104 us
    reduce_scatter x1, waiting for transfers between devices, local(): grad = lax.psum_scatter(grad, 'batch', scatter_dimension=0, tiled=True)  83.1 us
  transfers between devices with their start and end apart: 1, of which 1 were waited for; matrix products, arithmetic and copies ran while one was open for 0% of the time, Pallas kernels for 0%

profile of v1, /device:TPU:0, one launch (start us, length us, event | category | flops | bytes accessed | tf_op | source)
XLA Modules:
  0.0 201.7 jit_solution(6854575975469184690)
XLA Ops:
  7.2 0.0 reduce-scatter.2.cloned.1.call-start
  7.2 103.9 %shard_map.50 = (f32[8,128]{1,0:T(8,128)}, f32[256,8192]{1,0:T(8,128)}) custom-call(bf16[1024,256]{1,0:T(8,128)(2,1)} %te.1, bf16[1024,256]{1,0:T(8,128)(2,1)} %se.1, bf16[256,8192]{1,0:T(8,128)(2,1)} %pr.1), custom_call_target="tpu_custom_call" | custom-call | tf_op jit(solution)/shard_map/pallas_call | solution.py:234
  111.1 0.0 copy-start
  111.1 0.0 reduce-scatter.2.cloned.1.call-update
  111.2 83.1 %reduce-scatter.2.cloned.1.call-done = f32[16,8192]{1,0:T(8,128)} async-done(((f32[256,8192]{1,0:T(8,128)}), f32[16,8192]{1,0:T(8,128)}) %reduce-scatter.2.cloned.1.call-update) | async-done | bytes 524304 | tf_op jit(solution)/shard_map/reduce_scatter | solution.py:271
  194.3 0.0 copy-done
  194.3 0.6 copy.6
Async XLA Ops:
  7.2 187.1 %reduce-scatter.2.cloned.1.call-start = ((), (), s32[]{:S(2)}) async-start(), calls=%async_computation.1 | async-start | bytes 8912896 | tf_op jit(solution)/shard_map/reduce_scatter | solution.py:271
  111.1 83.2 %copy-start = (f32[8,128]{1,0:T(8,128)S(1)}, f32[8,128]{1,0:T(8,128)}, u32[]{:S(2)}) copy-start(f32[8,128]{1,0:T(8,128)} %get-tuple-element.4) | copy-start | bytes 12292
Sparse Core Ops, SparseCore 0:
  111.3 82.9 reduce-scatter.1

commit v2 on v0

v2 whole, which is shorter than its diff:
```python
import jax
import jax.numpy as jnp
from jax import lax
from jax.experimental import pallas as pl
from jax.experimental.pallas import tpu as pltpu
from jax.sharding import PartitionSpec as P

PROTOS = 65536
CROPS = 16384
ITERS = 3
TEACHER_TEMP = 0.07
STUDENT_TEMP = 0.1
NP = 8
NX = 4
ROWS = 1024
COLS = 8192
D = 256
MINE = COLS // NX
CH = 512
NQ = MINE // CH
HALF = CH // 2
FACTOR = PROTOS / (STUDENT_TEMP * CROPS)
LOG2E = 1.4426950408889634
MESH = pl.DeviceIdType.MESH
F32 = jnp.float32
BF16 = jnp.bfloat16


def unit(values, axis):
    wide = values.astype(F32)
    return (wide * lax.rsqrt(jnp.sum(wide * wide, axis=axis, keepdims=True) + 1e-06)).astype(BF16)


def rows_to_vec(part):
    out = []
    for i in range(8):
        block = part[pl.ds(i * 128, 128), :]
        out.append(jnp.sum(block.T, axis=0, keepdims=True))
    return jnp.concatenate(out, axis=0)


def vec_to_rows(vec, out):
    for i in range(8):
        out[pl.ds(i * 128, 128), :] = jnp.broadcast_to(vec[i : i + 1, :], (128, 128)).T


def send(src, dst, s, r, **where):
    pltpu.make_async_remote_copy(
        src_ref=src, dst_ref=dst, send_sem=s, recv_sem=r, device_id=where, device_id_type=MESH
    ).start()


def wait(some, sem):
    pltpu.make_async_copy(some, some, sem).wait()


def kernel(
    te, se, pr, loss, grad,
    ut4, us4, ust4, up, big, colv, cin, cb, rvec, row_in, az, az_in,
    land, mine, wa, pz, xp, gb, ring, tot, xv, xv_in,
    s_in, s_col, r_col, s_row, r_row, s_x, r_x, s_z, r_z, s_k, r_k, s_az, r_az,
    s_ring, r_ring, s_out, r_out, s_xv, r_xv,
):
    mb = lax.axis_index("batch")
    mp = lax.axis_index("proto")
    y, x = mb // NX, lax.rem(mb, NX)
    other = mp + 1 - 2 * lax.rem(mp, 2)
    wide, part = wa.at[0], wa.at[1]
    gg = big.at[pl.ds(0, D), pl.ds(0, MINE)]

    def at_x(d):
        return y * NX + lax.rem(x + d, NX)

    def at_y(d):
        return lax.rem(y + d, 4) * NX + x

    def at_z(d):
        return lax.rem(mp + 2 * d, NP)

    barrier = pltpu.get_barrier_semaphore()
    for d in (1, 2, 3):
        pl.semaphore_signal(barrier, inc=1, device_id={"batch": at_x(d)}, device_id_type=MESH)
        pl.semaphore_signal(barrier, inc=1, device_id={"batch": at_y(d)}, device_id_type=MESH)
    for d in range(1, NP):
        pl.semaphore_signal(barrier, inc=1, device_id={"proto": lax.rem(mp + d, NP)}, device_id_type=MESH)

    fetch = [pltpu.make_async_copy(te, ut4.at[0], s_in.at[0]), pltpu.make_async_copy(se, us4.at[0], s_in.at[1])]
    for j in range(4):
        cols = pl.ds(j * 2048, 2048)
        fetch.append(pltpu.make_async_copy(pr.at[:, cols], up.at[:, cols], s_in.at[2 + j]))
    for copy in fetch:
        copy.start()
    fetch[0].wait()
    ut4[0] = unit(ut4[0], 1)
    fetch[1].wait()
    us4[0] = unit(us4[0], 1)
    slab = pl.ds(pl.multiple_of(mp * 128, 128), 128)
    mine[0] = ut4[0, slab, :].astype(F32)
    mine[1] = us4[0, slab, :].astype(F32)
    pl.semaphore_wait(barrier, 6 + NP - 1)

    send(mine, land.at[mp, 2], s_x.at[0], r_x.at[0], batch=at_x(1))
    send(mine, land.at[mp, 0], s_x.at[1], r_x.at[1], batch=at_x(3))

    for j in range(4):
        fetch[2 + j].wait()

    def first(j, carry):
        for k in range(4):
            some = pl.ds(pl.multiple_of(j * 2048 + k * 512, 512), 512)
            up[:, some] = unit(up[:, some], 0)
        cols = pl.ds(pl.multiple_of(j * 2048, 2048), 2048)
        w = up[:, cols]
        total = jnp.zeros((8, 2048), F32)
        for i in range(8):
            rows = pl.ds(i * 128, 128)
            e = jnp.exp2(jnp.dot(ut4[0, rows, :], w, preferred_element_type=F32) * (LOG2E / TEACHER_TEMP))
            big[rows, cols] = e
            total = total + jnp.sum(e.reshape(16, 8, 2048), axis=0)
        flat = jnp.sum(total, axis=0, keepdims=True)
        for k in range(16):
            colv[0, 0, pl.ds(j * 16 + k, 1), :] = flat[:, k * 128 : (k + 1) * 128]
        return carry

    lax.fori_loop(0, 4, first, 0)

    def col_send(it, ph):
        src = colv.at[it, ph]
        for d in (2, 1, 3):
            for h in range(2):
                half = pl.ds(32 * h, 32)
                to = at_y(d) if h == ph else at_x(d)
                send(src.at[half], cin.at[it, ph, d - 1, half], s_col.at[it, ph], r_col.at[it, ph], batch=to)

    def col_recv(it, ph):
        wait(cin.at[it, ph], r_col.at[it, ph])
        colv[it, ph + 1] = colv[it, ph] + cin[it, ph, 0] + cin[it, ph, 1] + cin[it, ph, 2]

    def spread_cols(it):
        c = 1.0 / (colv[it, 2] * PROTOS)
        for j in range(64):
            cb[:, pl.ds(j * 128, 128)] = jnp.broadcast_to(c[j : j + 1, :], (8, 128))

    def row_pass():
        for g in range(4):
            c = [cb[:, pl.ds(g * 2048 + k * 128, 128)] for k in range(16)]

            def step(i, carry):
                for u in range(4):
                    rows = pl.ds(pl.multiple_of(i * 32 + u * 8, 8), 8)
                    acc = [big[rows, pl.ds(g * 2048 + k * 128, 128)] * c[k] for k in range(4)]
                    for k in range(4, 16):
                        acc[k % 4] = acc[k % 4] + big[rows, pl.ds(g * 2048 + k * 128, 128)] * c[k]
                    s = (acc[0] + acc[1]) + (acc[2] + acc[3])
                    part[rows, :] = s if g == 0 else part[rows, :] + s
                return carry

            lax.fori_loop(0, 32, step, 0)

    def col_pass(it):
        for g in range(4):
            def step(i, acc):
                acc = list(acc)
                for u in range(4):
                    rows = pl.ds(pl.multiple_of(i * 32 + u * 8, 8), 8)
                    a = wide[rows, :]
                    for k in range(16):
                        acc[k] = acc[k] + big[rows, pl.ds(g * 2048 + k * 128, 128)] * a
                return tuple(acc)

            acc = lax.fori_loop(0, 32, step, tuple(jnp.zeros((8, 128), F32) for _ in range(16)))
            for k in range(16):
                colv[it, 0, pl.ds(g * 16 + k, 1), :] = jnp.sum(acc[k], axis=0, keepdims=True)

    def row_send(src, dst, k):
        for d in (4, 3, 5, 2, 6, 7, 1):
            send(src, dst.at[mp], s_row.at[k], r_row.at[k], proto=lax.rem(mp + d, NP))

    def row_recv(src, dst, k):
        dst[mp] = src[...]
        wait(dst.at[pl.ds(0, NP - 1)], r_row.at[k])
        return jnp.sum(dst[...], axis=0)

    def student(lo, hi):
        def step(r, carry):
            rows = pl.ds(pl.multiple_of(r * 256, 256), 256)
            acc = jnp.zeros((256, 128), F32)
            for j in range(16):
                s = jnp.dot(us4[0, rows, :], up[:, pl.ds(j * 512, 512)], preferred_element_type=F32)
                e = jnp.exp2(s * (LOG2E / STUDENT_TEMP))
                for k in range(4):
                    acc = acc + e[:, k * 128 : (k + 1) * 128]
            xp[0, rows, :] = acc
            return carry

        lax.fori_loop(lo, hi, step, 0)

    def slabs(p):
        rows = pl.ds(pl.multiple_of(p * 128, 128), 128)
        for d in (1, 2, 3):
            ut4[d, rows, :] = land[p, d - 1, 0].astype(BF16)
            v = land[p, d - 1, 1]
            us4[d, rows, :] = v.astype(BF16)
            ust4[d, :, rows] = v.T.astype(BF16)

    z1, z3, z2 = at_z(1), at_z(3), at_z(2)

    col_send(0, 0)
    student(0, 2)
    col_recv(0, 0)
    col_send(0, 1)
    wait(mine, r_x.at[0])
    wait(mine, r_x.at[1])
    send(land.at[mp, 2, 0], land.at[mp, 1, 0], s_x.at[2], r_x.at[2], batch=at_x(1))
    send(land.at[mp, 0, 1], land.at[mp, 1, 1], s_x.at[3], r_x.at[3], batch=at_x(3))
    student(2, 4)
    rvec[3] = rows_to_vec(xp.at[0])
    col_recv(0, 1)
    spread_cols(0)
    row_pass()
    rvec[0] = rows_to_vec(part)
    row_send(rvec.at[0], row_in.at[0], 0)
    row_send(rvec.at[3], row_in.at[3], 3)
    wait(land.at[mp, 1, 0], r_x.at[2])
    wait(land.at[mp, 1, 1], r_x.at[3])
    send(land.at[mp, :, 0], land.at[mp, :, 0], s_z.at[0], r_z.at[0], proto=z1)
    send(land.at[mp, :, 0], land.at[mp, :, 0], s_z.at[1], r_z.at[1], proto=z3)
    send(land.at[mp, 0, 1], land.at[mp, 0, 1], s_z.at[2], r_z.at[2], proto=z1)
    send(land.at[mp, 0, 1], land.at[mp, 0, 1], s_z.at[3], r_z.at[3], proto=z3)
    send(land.at[mp], land.at[mp], s_k.at[0], r_k.at[0], proto=other)
    for i in range(8):
        block = us4[0, pl.ds(i * 128, 128), :]
        ust4[0, :, pl.ds(i * 128, 128)] = block.astype(F32).T.astype(BF16)
    total = row_recv(rvec.at[0], row_in.at[0], 0)
    vec_to_rows(1.0 / (total * CROPS), wide)

    col_pass(1)
    col_send(1, 0)
    z = row_recv(rvec.at[3], row_in.at[3], 3)
    az[0] = FACTOR / z
    slabs(mp)
    col_recv(1, 0)
    col_send(1, 1)
    col_recv(1, 1)
    spread_cols(1)
    row_pass()
    rvec[1] = rows_to_vec(part)
    row_send(rvec.at[1], row_in.at[1], 1)
    wait(land.at[mp, :, 0], r_z.at[0])
    wait(land.at[mp, :, 0], r_z.at[1])
    wait(land.at[mp, 0, 1], r_z.at[2])
    wait(land.at[mp, 0, 1], r_z.at[3])
    late = pl.ds(1, 2)
    send(land.at[z3, :, 0], land.at[z3, :, 0], s_z.at[4], r_z.at[4], proto=z1)
    send(land.at[mp, late, 1], land.at[mp, late, 1], s_z.at[5], r_z.at[5], proto=z3)
    send(land.at[mp, late, 1], land.at[mp, late, 1], s_z.at[6], r_z.at[6], proto=z1)
    wait(land.at[other], r_k.at[0])
    slabs(other)
    total = row_recv(rvec.at[1], row_in.at[1], 1)
    vec_to_rows(1.0 / (total * CROPS), wide)

    col_pass(2)
    col_send(2, 0)
    col_recv(2, 0)
    col_send(2, 1)
    wait(land.at[mp, late, 1], r_z.at[5])
    wait(land.at[mp, late, 1], r_z.at[6])
    send(land.at[z1, :, 1], land.at[z1, :, 1], s_z.at[7], r_z.at[7], proto=z3)
    send(land.at[z1], land.at[z1], s_k.at[1], r_k.at[1], proto=other)
    send(land.at[z3], land.at[z3], s_k.at[2], r_k.at[2], proto=other)
    slabs(z1)
    slabs(z3)
    col_recv(2, 1)
    spread_cols(2)
    row_pass()
    rvec[2] = rows_to_vec(part)
    row_send(rvec.at[2], row_in.at[2], 2)
    wait(land.at[z2, :, 0], r_z.at[4])
    wait(land.at[z2, :, 1], r_z.at[7])
    send(land.at[z2], land.at[z2], s_k.at[3], r_k.at[3], proto=other)
    slabs(z2)
    total = row_recv(rvec.at[2], row_in.at[2], 2)
    az[1] = FACTOR / total
    for d in (1, 2, 3):
        send(az, az_in.at[3 - d], s_az, r_az, batch=at_x(d))
    vec_to_rows(az[0], pz.at[0])
    vec_to_rows(az[1], wa.at[0])

    base = x * MINE

    def block(q, g):
        cols = pl.ds(pl.multiple_of(base + q * CH, CH), CH)
        w = up[:, cols]
        c = cb[pl.ds(0, 1), cols]
        n = CH // 128
        for b in range(4):
            rows = pl.ds(b * 256, 256)
            s = jnp.dot(us4[g, rows, :], w, preferred_element_type=F32)
            t = jnp.exp2(jnp.dot(ut4[g, rows, :], w, preferred_element_type=F32) * (LOG2E / TEACHER_TEMP))
            t = t * jnp.concatenate([wa[g, rows, :]] * n, axis=1) * c
            p = jnp.exp2(s * (LOG2E / STUDENT_TEMP)) * jnp.concatenate([pz[g, rows, :]] * n, axis=1)
            gb[rows, :] = (p - t).astype(BF16)
            ts = t * s
            ts = (ts[:, :128] + ts[:, 128:256]) + (ts[:, 256:384] + ts[:, 384:])
            xp[g, rows, :] = ts if q == 0 else xp[g, rows, :] + ts
        return jnp.dot(ust4[g], gb[...], preferred_element_type=F32)

    def ring_first(q):
        for h in range(2):
            lanes = pl.ds(q * CH + h * HALF, HALF)
            near, far = (1, 3) if h == 0 else (3, 1)
            opposite = pl.ds(pl.multiple_of(lax.rem(y + 2, 4) * 64, 64), 64)
            direct = pl.ds(pl.multiple_of(lax.rem(y + near, 4) * 64, 64), 64)
            send(gg.at[opposite, lanes], ring.at[q, h, 0], s_ring.at[q, h, 0], r_ring.at[q, h, 0], batch=at_y(far))
            send(gg.at[direct, lanes], ring.at[q, h, 1], s_ring.at[q, h, 1], r_ring.at[q, h, 1], batch=at_y(near))

    def ring_second(q):
        for h in range(2):
            lanes = pl.ds(q * CH + h * HALF, HALF)
            far = 3 if h == 0 else 1
            theirs = pl.ds(pl.multiple_of(lax.rem(y + far, 4) * 64, 64), 64)
            wait(ring.at[q, h, 0], r_ring.at[q, h, 0])
            ring[q, h, 0] = ring[q, h, 0] + gg[theirs, lanes]
            send(ring.at[q, h, 0], ring.at[q, h, 2], s_ring.at[q, h, 2], r_ring.at[q, h, 2], batch=at_y(far))

    def ring_last(q):
        rows = pl.ds(pl.multiple_of(y * 64, 64), 64)
        for h in range(2):
            lanes = pl.ds(q * CH + h * HALF, HALF)
            wait(ring.at[q, h, 1], r_ring.at[q, h, 1])
            wait(ring.at[q, h, 2], r_ring.at[q, h, 2])
            tot[q, :, pl.ds(h * HALF, HALF)] = gg[rows, lanes] + ring[q, h, 1] + ring[q, h, 2]
        cols = pl.ds(pl.multiple_of(base + q * CH, CH), CH)
        for d in (2, 1, 3):
            to = lax.rem(x + d, NX)
            send(tot.at[q, pl.ds(pl.multiple_of(to * 16, 16), 16)], grad.at[:, cols], s_out, r_out, batch=at_x(d))
        grad[:, cols] = tot[q, pl.ds(pl.multiple_of(x * 16, 16), 16)]

    for q in range(NQ):
        lanes = pl.ds(q * CH, CH)
        gg[:, lanes] = block(q, 0)
        if q == 0:
            for k, p in ((1, at_z(1)), (2, at_z(3)), (3, at_z(2))):
                theirs = p + 1 - 2 * lax.rem(p, 2)
                wait(land.at[theirs], r_k.at[k])
                slabs(theirs)
            wait(az_in, r_az)
            for g in (1, 2, 3):
                vec_to_rows(az_in[g - 1, 0], pz.at[g])
                vec_to_rows(az_in[g - 1, 1], wa.at[g])

        def more(g, carry):
            gg[:, lanes] += block(q, g)
            return carry

        lax.fori_loop(1, 4, more, 0)
        ring_first(q)
        if q >= 1:
            ring_second(q - 1)
        if q >= 2:
            ring_last(q - 2)
    for g in range(4):
        xv[g] = rows_to_vec(xp.at[g])
    for d in (1, 2, 3):
        send(xv.at[d], xv_in.at[3 - d], s_xv, r_xv, batch=at_x(d))
    ring_second(NQ - 1)
    ring_last(NQ - 2)
    wait(xv_in, r_xv)
    rvec[4] = (xv[0] + xv_in[0] + xv_in[1] + xv_in[2]) * (1.0 / (FACTOR * STUDENT_TEMP))
    row_send(rvec.at[4], row_in.at[4], 4)
    ring_last(NQ - 1)
    cross = row_recv(rvec.at[4], row_in.at[4], 4)
    loss[...] = jnp.log(z) - cross

    wait(grad.at[:, pl.ds(0, 3 * MINE)], r_out)
    wait(grad.at[:, pl.ds(0, 3 * MINE)], s_out)
    for it in range(ITERS):
        for ph in range(2):
            wait(cin.at[it, ph], s_col.at[it, ph])
    for k in range(5):
        wait(row_in.at[k, pl.ds(0, NP - 1)], s_row.at[k])
    for k in range(2):
        wait(mine, s_x.at[k])
        wait(mine.at[0], s_x.at[2 + k])
    for k, some in (
        (0, land.at[mp, :, 0]), (1, land.at[mp, :, 0]), (2, land.at[mp, 0, 0]), (3, land.at[mp, 0, 0]),
        (4, land.at[mp, :, 0]), (5, land.at[mp, late, 0]), (6, land.at[mp, late, 0]), (7, land.at[mp, :, 0]),
    ):
        wait(some, s_z.at[k])
    for k in range(4):
        wait(land.at[mp], s_k.at[k])
    wait(az_in, s_az)
    wait(xv_in, s_xv)
    for q in range(NQ):
        for h in range(2):
            for k in range(3):
                wait(ring.at[q, h, k], s_ring.at[q, h, k])


def local(teacher_emb, student_emb, prototypes):
    vmem = pl.BlockSpec(memory_space=pltpu.VMEM)
    hbm = pl.BlockSpec(memory_space=pl.ANY)
    dma = pltpu.SemaphoreType.DMA
    loss, grad = pl.pallas_call(
        kernel,
        out_shape=(
            jax.ShapeDtypeStruct((8, 128), F32),
            jax.ShapeDtypeStruct((16, COLS), F32),
        ),
        in_specs=[hbm] * 3,
        out_specs=(vmem, vmem),
        scratch_shapes=[
            pltpu.VMEM((NX, ROWS, D), BF16),
            pltpu.VMEM((NX, ROWS, D), BF16),
            pltpu.VMEM((NX, D, ROWS), BF16),
            pltpu.VMEM((D, COLS), BF16),
            pltpu.VMEM((ROWS, COLS), F32),
            pltpu.VMEM((ITERS, 3, 64, 128), F32),
            pltpu.VMEM((ITERS, 2, 3, 64, 128), F32),
            pltpu.VMEM((8, COLS), F32),
            pltpu.VMEM((5, 8, 128), F32),
            pltpu.VMEM((5, NP, 8, 128), F32),
            pltpu.VMEM((2, 8, 128), F32),
            pltpu.VMEM((3, 2, 8, 128), F32),
            pltpu.VMEM((NP, 3, 2, 128, D), F32),
            pltpu.VMEM((2, 128, D), F32),
            pltpu.VMEM((NX, ROWS, 128), F32),
            pltpu.VMEM((NX, ROWS, 128), F32),
            pltpu.VMEM((NX, ROWS, 128), F32),
            pltpu.VMEM((ROWS, CH), BF16),
            pltpu.VMEM((NQ, 2, 3, 64, HALF), F32),
            pltpu.VMEM((NQ, 64, CH), F32),
            pltpu.VMEM((NX, 8, 128), F32),
            pltpu.VMEM((3, 8, 128), F32),
            dma((6,)),
            dma((ITERS, 2)), dma((ITERS, 2)),
            dma((5,)), dma((5,)),
            dma((4,)), dma((4,)),
            dma((8,)), dma((8,)),
            dma((4,)), dma((4,)),
            dma, dma,
            dma((NQ, 2, 3)), dma((NQ, 2, 3)),
            dma, dma,
            dma, dma,
        ],
        compiler_params=pltpu.CompilerParams(
            collective_id=0, has_side_effects=True, vmem_limit_bytes=63 * 1024 * 1024
        ),
    )(teacher_emb, student_emb, prototypes)
    return loss.reshape(ROWS), grad


def solution(mesh):
    in_specs = (P("batch", None), P("batch", None), P(None, "proto"))
    out_specs = (P("batch"), P("batch", "proto"))
    return jax.shard_map(local, mesh=mesh, in_specs=in_specs, out_specs=out_specs, check_vma=False)
```

time: 508 us -> 111 us (0.22)
  blocking collectives: 265 us -> 0 us
  Pallas kernels: 0 us -> 107 us
  waiting for transfers between devices: 78.5 us -> 0 us
  other arithmetic: 75.6 us -> 0 us
  matrix products: 73.8 us -> 0 us
  between operations: 14.1 us -> 0.64 us
    psum x7 -> x0, blocking collectives: 265 us -> none  [the longest x3 214 us: local(): proto_shift = -math.log(PROTOS) - jnp.log(lax.psum(col_local, 'batch'))]
    pallas_call x0 -> x1, Pallas kernels: none -> 107 us  [local(): pl.pallas_call(kernel, out_shape=(jax.ShapeDtypeStruct((8, 128), F32), ja...]
    reduce_scatter x1 -> x0, waiting for transfers between devices: 78.5 us -> none  [local(): lax.psum_scatter(lax.dot_general(unit_student, grad_scaled, (((0,), (0,))...]
    reduce_sum x8 -> x0, other arithmetic: 75 us -> none  [the longest x3 41.4 us: local(): row_local = jnp.sum(jnp.exp(teacher + proto_shift[None, :]), axis=1)]
    dot_general x3 -> x0, matrix products: 73.8 us -> none  [the longest x1 29.7 us: local(): jnp.dot(unit_student, unit_protos, preferred_element_type=jnp.float32)]
  transfers between devices with their start and end apart: 1 -> 0, of which waited for: 1 -> 0; matrix products, arithmetic and copies ran while one was open for 0% -> 0% of each run, Pallas kernels for 0% -> 0%
where the time goes in v2:
time: 111 us
  Pallas kernels  107 us (96%)
  local copies, waits for them, and re-layouts  3.14 us (3%)
    pallas_call x1, Pallas kernels, local(): pl.pallas_call(kernel, out_shape=(jax.ShapeDtypeStruct((8, 128), F32), ja...  107 us
    unnamed x2, local copies, waits for them, and re-layouts  3.14 us

profile of v2, /device:TPU:0, one launch (start us, length us, event | category | flops | bytes accessed | tf_op | source)
XLA Modules:
  0.0 110.9 jit_solution(15473652292839355017)
XLA Ops:
  0.6 107.1 %shard_map.50 = (f32[8,128]{1,0:T(8,128)}, f32[16,8192]{1,0:T(8,128)}) custom-call(bf16[1024,256]{1,0:T(8,128)(2,1)} %te.1, bf16[1024,256]{1,0:T(8,128)(2,1)} %se.1, bf16[256,8192]{1,0:T(8,128)(2,1)} %pr.1), custom_call_target="tpu_custom_call" | custom-call | tf_op jit(solution)/shard_map/pallas_call | solution.py:404
  107.7 1.3 %copy.7 = f32[1024]{0:T(1024)} copy(f32[1024]{0:T(1024)} %bitcast.1) | data formatting | bytes 8192
  109.0 1.9 %copy.8 = f32[16,8192]{1,0:T(8,128)} copy(f32[16,8192]{1,0:T(8,128)} %get-tuple-element.9) | data formatting | bytes 1048576

commit v3 on v2

v3 whole, which is shorter than its diff:
```python
import jax
import jax.numpy as jnp
from jax import lax
from jax.experimental import pallas as pl
from jax.experimental.pallas import tpu as pltpu
from jax.sharding import PartitionSpec as P

PROTOS = 65536
CROPS = 16384
ITERS = 3
TEACHER_TEMP = 0.07
STUDENT_TEMP = 0.1
NP = 8
NX = 4
ROWS = 1024
COLS = 8192
D = 256
MINE = COLS // NX
CH = 512
NQ = MINE // CH
HALF = CH // 2
FACTOR = PROTOS / (STUDENT_TEMP * CROPS)
LOG2E = 1.4426950408889634
MESH = pl.DeviceIdType.MESH
F32 = jnp.float32
BF16 = jnp.bfloat16


def unit(values, axis):
    wide = values.astype(F32)
    return (wide * lax.rsqrt(jnp.sum(wide * wide, axis=axis, keepdims=True) + 1e-06)).astype(BF16)


def rows_to_vec(part):
    out = []
    for i in range(8):
        block = part[pl.ds(i * 128, 128), :]
        out.append(jnp.sum(block.T, axis=0, keepdims=True))
    return jnp.concatenate(out, axis=0)


def vec_to_rows(vec, out):
    for i in range(8):
        out[pl.ds(i * 128, 128), :] = jnp.broadcast_to(vec[i : i + 1, :], (128, 128)).T


def send(src, dst, s, r, **where):
    pltpu.make_async_remote_copy(
        src_ref=src, dst_ref=dst, send_sem=s, recv_sem=r, device_id=where, device_id_type=MESH
    ).start()


def wait(some, sem):
    pltpu.make_async_copy(some, some, sem).wait()


def kernel(
    te, se, pr, loss, grad,
    ut, us, ust, up, big, colv, cin, cb, rvec, row_in, az, az_in,
    land, mine, pz, gb, ring,
    s_in, s_col, r_col, s_row, r_row, s_x, r_x, s_z, r_z, s_k, r_k, s_az, r_az,
    s_ring, r_ring, s_out, r_out,
):
    mb = lax.axis_index("batch")
    mp = lax.axis_index("proto")
    y, x = mb // NX, lax.rem(mb, NX)
    other = mp + 1 - 2 * lax.rem(mp, 2)
    gg = big.at[pl.ds(0, D), pl.ds(0, MINE)]
    wa = [big.at[:, pl.ds(MINE + 128 * d, 128)] for d in range(4)]
    ut0, us0 = gb.at[pl.ds(0, ROWS), pl.ds(0, D)], gb.at[pl.ds(ROWS, ROWS), pl.ds(0, D)]
    wide, part, xp = pz.at[1], pz.at[2], pz.at[3]

    def at_x(d):
        return y * NX + lax.rem(x + d, NX)

    def at_y(d):
        return lax.rem(y + d, 4) * NX + x

    def at_z(d):
        return lax.rem(mp + 2 * d, NP)

    barrier = pltpu.get_barrier_semaphore()
    for d in (1, 2, 3):
        pl.semaphore_signal(barrier, inc=1, device_id={"batch": at_x(d)}, device_id_type=MESH)
        pl.semaphore_signal(barrier, inc=1, device_id={"batch": at_y(d)}, device_id_type=MESH)
    for d in range(1, NP):
        pl.semaphore_signal(barrier, inc=1, device_id={"proto": lax.rem(mp + d, NP)}, device_id_type=MESH)

    fetch = [pltpu.make_async_copy(te, ut0, s_in.at[0]), pltpu.make_async_copy(se, us0, s_in.at[1])]
    for j in range(4):
        cols = pl.ds(j * 2048, 2048)
        fetch.append(pltpu.make_async_copy(pr.at[:, cols], up.at[:, cols], s_in.at[2 + j]))
    for copy in fetch:
        copy.start()
    fetch[0].wait()
    ut0[...] = unit(ut0[...], 1)
    fetch[1].wait()
    us0[...] = unit(us0[...], 1)
    slab = pl.ds(pl.multiple_of(mp * 128, 128), 128)
    mine[0, 0] = ut0[slab, :].astype(F32)
    mine[0, 1] = us0[slab, :].astype(F32)
    pl.semaphore_wait(barrier, 6 + NP - 1)

    def x_near(i, p):
        send(mine.at[i], land.at[p, 2], s_x.at[i, 0], r_x.at[i, 0], batch=at_x(1))
        send(mine.at[i], land.at[p, 0], s_x.at[i, 1], r_x.at[i, 1], batch=at_x(3))

    def x_far(i, p):
        wait(mine.at[0], r_x.at[i, 0])
        wait(mine.at[0], r_x.at[i, 1])
        send(land.at[p, 2, 0], land.at[p, 1, 0], s_x.at[i, 2], r_x.at[i, 2], batch=at_x(1))
        send(land.at[p, 0, 1], land.at[p, 1, 1], s_x.at[i, 3], r_x.at[i, 3], batch=at_x(3))

    def x_done(i, p):
        wait(land.at[p, 1, 0], r_x.at[i, 2])
        wait(land.at[p, 1, 1], r_x.at[i, 3])

    x_near(0, mp)

    def col_send(it, ph, k):
        on_x = lax.rem(k + ph, 2)
        on_y = 1 - on_x
        for d in (2, 1, 3):
            to = lax.rem(y + d * on_y, 4) * NX + lax.rem(x + d * on_x, NX)
            send(colv.at[it, ph, k], cin.at[it, ph, k, d - 1], s_col.at[it, ph, k], r_col.at[it, ph, k], batch=to)

    def col_recv(it, ph, k):
        wait(cin.at[it, ph, k], r_col.at[it, ph, k])
        colv[it, ph + 1, k] = colv[it, ph, k] + cin[it, ph, k, 0] + cin[it, ph, k, 1] + cin[it, ph, k, 2]

    def first(j, carry):
        cols = pl.ds(pl.multiple_of(j * 2048, 2048), 2048)
        pltpu.make_async_copy(pr.at[:, cols], up.at[:, cols], s_in.at[2 + j]).wait()
        for k in range(4):
            some = pl.ds(pl.multiple_of(j * 2048 + k * 512, 512), 512)
            up[:, some] = unit(up[:, some], 0)
        w = up[:, cols]
        total = jnp.zeros((8, 2048), F32)
        for i in range(8):
            rows = pl.ds(i * 128, 128)
            e = jnp.exp2(jnp.dot(ut0[rows, :], w, preferred_element_type=F32) * (LOG2E / TEACHER_TEMP))
            big[rows, cols] = e
            total = total + jnp.sum(e.reshape(16, 8, 2048), axis=0)
        flat = jnp.sum(total, axis=0, keepdims=True)
        for k in range(16):
            colv[0, 0, j, pl.ds(k, 1), :] = flat[:, k * 128 : (k + 1) * 128]
        col_send(0, 0, j)
        return carry

    lax.fori_loop(0, 4, first, 0)

    def row_pass(it, g):
        v = 1.0 / (colv[it, 2, g] * PROTOS)
        for j in range(16):
            cb[:, pl.ds((g * 16 + j) * 128, 128)] = jnp.broadcast_to(v[j : j + 1, :], (8, 128))
        c = [cb[:, pl.ds((g * 16 + k) * 128, 128)] for k in range(16)]

        def step(i, carry):
            res = []
            for u in range(16):
                rows = pl.ds(pl.multiple_of(i * 128, 128) + u * 8, 8)
                acc = [big[rows, pl.ds(g * 2048 + k * 128, 128)] * c[k] for k in range(4)]
                for k in range(4, 16):
                    acc[k % 4] = acc[k % 4] + big[rows, pl.ds(g * 2048 + k * 128, 128)] * c[k]
                total = (acc[0] + acc[1]) + (acc[2] + acc[3])
                res.append(total if g == 0 else part[rows, :] + total)
            for u in range(16):
                part[pl.ds(pl.multiple_of(i * 128, 128) + u * 8, 8), :] = res[u]
            return carry

        lax.fori_loop(0, 8, step, 0)

    def col_pass(it):
        for g in range(4):
            def step(i, acc):
                acc = list(acc)
                for u in range(4):
                    rows = pl.ds(pl.multiple_of(i * 32, 32) + u * 8, 8)
                    a = wide[rows, :]
                    for k in range(16):
                        acc[k] = acc[k] + big[rows, pl.ds(g * 2048 + k * 128, 128)] * a
                return tuple(acc)

            acc = lax.fori_loop(0, 32, step, tuple(jnp.zeros((8, 128), F32) for _ in range(16)))
            for k in range(16):
                colv[it, 0, g, pl.ds(k, 1), :] = jnp.sum(acc[k], axis=0, keepdims=True)
            col_send(it, 0, g)

    def row_send(src, dst, k):
        for d in (4, 3, 5, 2, 6, 7, 1):
            send(src, dst.at[mp], s_row.at[k], r_row.at[k], proto=lax.rem(mp + d, NP))

    def row_recv(src, dst, k):
        dst[mp] = src[...]
        wait(dst.at[pl.ds(0, NP - 1)], r_row.at[k])
        return jnp.sum(dst[...], axis=0)

    def student(r):
        rows = pl.ds(r * 256, 256)
        acc = jnp.zeros((256, 128), F32)
        for j in range(16):
            s = jnp.dot(us0[rows, :], up[:, pl.ds(j * 512, 512)], preferred_element_type=F32)
            e = jnp.exp2(s * (LOG2E / STUDENT_TEMP))
            for k in range(4):
                acc = acc + e[:, k * 128 : (k + 1) * 128]
        xp[rows, :] = acc

    def cross(lo, hi):
        def step(r, carry):
            rows = pl.ds(pl.multiple_of(r * 256, 256), 256)
            v = jnp.zeros((256, D), F32)
            for g in range(4):
                cols = pl.ds(g * 2048, 2048)
                kc = (big[rows, cols] * cb[pl.ds(0, 1), cols]).astype(BF16)
                v = v + lax.dot_general(kc, up[:, cols], (((1,), (1,)), ((), ())), preferred_element_type=F32)
            v = v * us0[rows, :].astype(F32)
            part[rows, :] = v[:, :128] + v[:, 128:]
            return carry

        lax.fori_loop(lo, hi, step, 0)

    def slabs(p):
        for d in (1, 2, 3):
            rows = pl.ds(pl.multiple_of(p * 512, 512) + d * 128, 128)
            cols = pl.ds(pl.multiple_of(p * 512 + d * 128, 128), 128)
            ut[rows, :] = land[p, d - 1, 0].astype(BF16)
            v = land[p, d - 1, 1]
            us[rows, :] = v.astype(BF16)
            ust[:, cols] = v.T.astype(BF16)

    z1, z3, z2 = at_z(1), at_z(3), at_z(2)

    col_recv(0, 0, 0)
    col_send(0, 1, 0)
    student(0)
    col_recv(0, 0, 1)
    col_send(0, 1, 1)
    col_recv(0, 0, 2)
    col_send(0, 1, 2)
    student(1)
    col_recv(0, 0, 3)
    col_send(0, 1, 3)
    x_far(0, mp)
    for k in range(4):
        col_recv(0, 1, k)
        row_pass(0, k)
    rvec[0] = rows_to_vec(part)
    row_send(rvec.at[0], row_in.at[0], 0)
    x_done(0, mp)
    most = pl.ds(0, 2)
    for k, to in ((0, z1), (1, z3)):
        send(land.at[mp, :, 0], land.at[mp, :, 0], s_z.at[0, k], r_z.at[0, k], proto=to)
    for k, to in ((0, z1), (1, z3)):
        send(land.at[mp, most, 1], land.at[mp, most, 1], s_z.at[1, k], r_z.at[1, k], proto=to)
    send(land.at[mp], land.at[mp], s_k.at[0], r_k.at[0], proto=other)
    slab = pl.ds(pl.multiple_of(z2 * 128, 128), 128)
    mine[1, 0] = ut0[slab, :].astype(F32)
    mine[1, 1] = us0[slab, :].astype(F32)
    x_near(1, z2)
    student(2)
    student(3)
    rvec[3] = rows_to_vec(xp)
    total = row_recv(rvec.at[0], row_in.at[0], 0)
    vec_to_rows(1.0 / (total * CROPS), wide)

    col_pass(1)
    for i in range(8):
        v = us0[pl.ds(i * 128, 128), :]
        us[pl.ds(i * 512, 128), :] = v
        ust[:, pl.ds(i * 512, 128)] = v.astype(F32).T.astype(BF16)
        ut[pl.ds(i * 512, 128), :] = ut0[pl.ds(i * 128, 128), :]
    slabs(mp)
    for k in range(4):
        col_recv(1, 0, k)
        col_send(1, 1, k)
    for k in range(4):
        col_recv(1, 1, k)
        row_pass(1, k)
    rvec[1] = rows_to_vec(part)
    row_send(rvec.at[1], row_in.at[1], 1)
    row_send(rvec.at[3], row_in.at[3], 3)
    for k, to in ((0, z1), (1, z3)):
        send(land.at[mp, 2, 1], land.at[mp, 2, 1], s_z.at[2, k], r_z.at[2, k], proto=to)
    x_far(1, z2)
    wait(land.at[other], r_k.at[0])
    slabs(other)
    total = row_recv(rvec.at[1], row_in.at[1], 1)
    vec_to_rows(1.0 / (total * CROPS), wide)

    col_pass(2)
    z = row_recv(rvec.at[3], row_in.at[3], 3)
    az[0] = FACTOR / z
    for d in (1, 2, 3):
        send(az.at[0], az_in.at[0, 3 - d], s_az.at[0], r_az.at[0], batch=at_x(d))
    for k in range(2):
        wait(land.at[mp, :, 0], r_z.at[0, k])
        wait(land.at[mp, most, 1], r_z.at[1, k])
        wait(land.at[mp, 2, 1], r_z.at[2, k])
    x_done(1, z2)
    for k, p in ((1, z1), (2, z3), (3, z2)):
        send(land.at[p], land.at[p], s_k.at[k], r_k.at[k], proto=other)
    for k in range(4):
        col_recv(2, 0, k)
        col_send(2, 1, k)
    wait(az_in.at[0], r_az.at[0])
    vec_to_rows(az[0], pz.at[0])
    vec_to_rows(az_in[0, 0], pz.at[1])
    vec_to_rows(az_in[0, 2], pz.at[3])
    for k in range(4):
        col_recv(2, 1, k)
        row_pass(2, k)
    rvec[2] = rows_to_vec(part)
    row_send(rvec.at[2], row_in.at[2], 2)
    slabs(z1)
    slabs(z3)
    slabs(z2)
    for k, p in ((1, z1), (2, z3), (3, z2)):
        theirs = p + 1 - 2 * lax.rem(p, 2)
        wait(land.at[theirs], r_k.at[k])
        slabs(theirs)
    cross(0, 2)
    total = row_recv(rvec.at[2], row_in.at[2], 2)
    az[1] = FACTOR / total
    for d in (1, 2, 3):
        send(az.at[1], az_in.at[1, 3 - d], s_az.at[1], r_az.at[1], batch=at_x(d))
    cross(2, 4)
    rvec[4] = rows_to_vec(part) / (total * STUDENT_TEMP)
    row_send(rvec.at[4], row_in.at[4], 4)
    vec_to_rows(az[1], wa[0])
    vec_to_rows(az_in[0, 1], pz.at[2])
    wait(az_in.at[1], r_az.at[1])
    for g in (1, 2, 3):
        vec_to_rows(az_in[1, g - 1], wa[g])

    base = x * MINE

    def block(q):
        cols = pl.ds(pl.multiple_of(base + q * CH, CH), CH)
        w = up[:, cols]
        c = cb[pl.ds(0, 1), cols]
        n = CH // 128
        for p in range(8):
            rows = pl.ds(p * 512, 512)
            own = pl.ds(p * 128, 128)
            s = jnp.dot(us[rows, :], w, preferred_element_type=F32)
            t = jnp.dot(ut[rows, :], w, preferred_element_type=F32)
            a = jnp.concatenate([wa[d][own, :] for d in range(4)], axis=0)
            e = jnp.concatenate([pz[d, own, :] for d in range(4)], axis=0)
            t = jnp.exp2(t * (LOG2E / TEACHER_TEMP)) * jnp.concatenate([a] * n, axis=1) * c
            s = jnp.exp2(s * (LOG2E / STUDENT_TEMP)) * jnp.concatenate([e] * n, axis=1)
            gb[rows, :] = (s - t).astype(BF16)
        gg[:, pl.ds(pl.multiple_of(q * CH, CH), CH)] = jnp.dot(ust[...], gb[...], preferred_element_type=F32)

    def lanes_of(q, h):
        return pl.ds(pl.multiple_of(q * CH + h * HALF, HALF), HALF)

    def rows_of(d):
        return pl.ds(pl.multiple_of(lax.rem(y + d, 4) * 64, 64), 64)

    def ring_first(q):
        for h in range(2):
            near, far = (1, 3) if h == 0 else (3, 1)
            send(gg.at[rows_of(2), lanes_of(q, h)], ring.at[q, h, 0], s_ring.at[q, h, 0], r_ring.at[q, h, 0], batch=at_y(far))
            send(gg.at[rows_of(near), lanes_of(q, h)], ring.at[q, h, 1], s_ring.at[q, h, 1], r_ring.at[q, h, 1], batch=at_y(near))

    def ring_second(q):
        for h in range(2):
            far = 3 if h == 0 else 1
            wait(ring.at[q, h, 0], r_ring.at[q, h, 0])
            ring[q, h, 0] = ring[q, h, 0] + gg[rows_of(far), lanes_of(q, h)]
            send(ring.at[q, h, 0], ring.at[q, h, 2], s_ring.at[q, h, 2], r_ring.at[q, h, 2], batch=at_y(far))

    def ring_last(q):
        for h in range(2):
            wait(ring.at[q, h, 1], r_ring.at[q, h, 1])
            wait(ring.at[q, h, 2], r_ring.at[q, h, 2])
            ring[q, h, 1] = gg[rows_of(0), lanes_of(q, h)] + ring[q, h, 1] + ring[q, h, 2]
            cols = pl.ds(pl.multiple_of(base + q * CH + h * HALF, HALF), HALF)
            for d in (2, 1, 3):
                to = pl.ds(pl.multiple_of(lax.rem(x + d, NX) * 16, 16), 16)
                send(ring.at[q, h, 1, to], grad.at[:, cols], s_out, r_out, batch=at_x(d))
            grad[:, cols] = ring[q, h, 1, pl.ds(pl.multiple_of(x * 16, 16), 16)]

    def last(q, carry):
        @pl.when(q < NQ)
        def _():
            block(q)
            ring_first(q)

        @pl.when((q >= 1) & (q <= NQ))
        def _():
            ring_second(q - 1)

        @pl.when(q >= 2)
        def _():
            ring_last(q - 2)

        return carry

    lax.fori_loop(0, NQ + 2, last, 0)
    loss[...] = jnp.log(z) - row_recv(rvec.at[4], row_in.at[4], 4)

    wait(grad.at[:, pl.ds(0, 3 * MINE)], r_out)
    wait(grad.at[:, pl.ds(0, 3 * MINE)], s_out)
    for it in range(ITERS):
        for ph in range(2):
            for k in range(4):
                wait(cin.at[it, ph, k], s_col.at[it, ph, k])
    for k in range(5):
        wait(row_in.at[k, pl.ds(0, NP - 1)], s_row.at[k])
    for i in range(2):
        for k in range(2):
            wait(mine.at[0], s_x.at[i, k])
            wait(mine.at[0, 0], s_x.at[i, 2 + k])
    for k in range(2):
        wait(land.at[mp, :, 0], s_z.at[0, k])
        wait(land.at[mp, most, 1], s_z.at[1, k])
        wait(land.at[mp, 2, 1], s_z.at[2, k])
    for k in range(4):
        wait(land.at[mp], s_k.at[k])
    for k in range(2):
        wait(az_in.at[k], s_az.at[k])
    for q in range(NQ):
        for h in range(2):
            for k in range(3):
                wait(ring.at[q, h, k], s_ring.at[q, h, k])


def handover(loss, grad, loss_out, grad_out):
    loss_out[...] = loss[...]
    grad_out[...] = grad[...]


def local(teacher_emb, student_emb, prototypes):
    vmem = pl.BlockSpec(memory_space=pltpu.VMEM)
    hbm = pl.BlockSpec(memory_space=pl.ANY)
    dma = pltpu.SemaphoreType.DMA
    loss, grad = pl.pallas_call(
        kernel,
        out_shape=(
            jax.ShapeDtypeStruct((8, 128), F32),
            jax.ShapeDtypeStruct((16, COLS), F32),
        ),
        in_specs=[hbm] * 3,
        out_specs=(vmem, vmem),
        scratch_shapes=[
            pltpu.VMEM((NX * ROWS, D), BF16),
            pltpu.VMEM((NX * ROWS, D), BF16),
            pltpu.VMEM((D, NX * ROWS), BF16),
            pltpu.VMEM((D, COLS), BF16),
            pltpu.VMEM((ROWS, COLS), F32),
            pltpu.VMEM((ITERS, 3, 4, 16, 128), F32),
            pltpu.VMEM((ITERS, 2, 4, 3, 16, 128), F32),
            pltpu.VMEM((8, COLS), F32),
            pltpu.VMEM((5, 8, 128), F32),
            pltpu.VMEM((5, NP, 8, 128), F32),
            pltpu.VMEM((2, 8, 128), F32),
            pltpu.VMEM((2, 3, 8, 128), F32),
            pltpu.VMEM((NP, 3, 2, 128, D), F32),
            pltpu.VMEM((2, 2, 128, D), F32),
            pltpu.VMEM((NX, ROWS, 128), F32),
            pltpu.VMEM((NX * ROWS, CH), BF16),
            pltpu.VMEM((NQ, 2, 3, 64, HALF), F32),
            dma((6,)),
            dma((ITERS, 2, 4)), dma((ITERS, 2, 4)),
            dma((5,)), dma((5,)),
            dma((2, 4)), dma((2, 4)),
            dma((3, 2)), dma((3, 2)),
            dma((4,)), dma((4,)),
            dma((2,)), dma((2,)),
            dma((NQ, 2, 3)), dma((NQ, 2, 3)),
            dma, dma,
        ],
        compiler_params=pltpu.CompilerParams(
            collective_id=0, has_side_effects=True, vmem_limit_bytes=63 * 1024 * 1024
        ),
    )(teacher_emb, student_emb, prototypes)
    loss, grad = pl.pallas_call(
        handover,
        out_shape=(
            jax.ShapeDtypeStruct((8, 128), F32),
            jax.ShapeDtypeStruct((16, COLS), F32),
        ),
        in_specs=[vmem] * 2,
        out_specs=(vmem, vmem),
    )(loss, grad)
    return loss.reshape(ROWS), grad


def solution(mesh):
    in_specs = (P("batch", None), P("batch", None), P(None, "proto"))
    out_specs = (P("batch"), P("batch", "proto"))
    return jax.shard_map(local, mesh=mesh, in_specs=in_specs, out_specs=out_specs, check_vma=False)
```

time: 111 us -> 94.4 us (0.85)
  Pallas kernels: 107 us -> 93.3 us
  local copies, waits for them, and re-layouts: 3.14 us -> 0 us
    pallas_call x1, Pallas kernels: 107 us -> 91.4 us  [local(): pl.pallas_call(kernel, out_shape=(jax.ShapeDtypeStruct((8, 128), F32), ja...]
    unnamed x2 -> x0, local copies, waits for them, and re-layouts: 3.14 us -> none
    pallas_call x0 -> x1, Pallas kernels: none -> 1.88 us  [local(): pl.pallas_call(handover, out_shape=(jax.ShapeDtypeStruct((8, 128), F32),...]
where the time goes in v3:
time: 94.4 us; the launch traced here: 93.9 us
  Pallas kernels  93.3 us (99%)
    pallas_call x1, Pallas kernels, local(): pl.pallas_call(kernel, out_shape=(jax.ShapeDtypeStruct((8, 128), F32), ja...  91.4 us

profile of v3, /device:TPU:0, one launch (start us, length us, event | category | flops | bytes accessed | tf_op | source)
XLA Modules:
  0.0 93.9 jit_solution(9334546878496452731)
XLA Ops:
  0.6 91.4 %shard_map.50 = (f32[8,128]{1,0:T(8,128)}, f32[16,8192]{1,0:T(8,128)}) custom-call(bf16[1024,256]{1,0:T(8,128)(2,1)} %te.1, bf16[1024,256]{1,0:T(8,128)(2,1)} %se.1, bf16[256,8192]{1,0:T(8,128)(2,1)} %pr.1), custom_call_target="tpu_custom_call" | custom-call | tf_op jit(solution)/shard_map/pallas_call | solution.py:438
  92.0 1.9 %shard_map.51 = (f32[8,128]{1,0:T(8,128)}, f32[16,8192]{1,0:T(8,128)}) custom-call(f32[8,128]{1,0:T(8,128)} %get-tuple-element.6.loss, f32[16,8192]{1,0:T(8,128)} %get-tuple-element.7.grad), custom_call_target="tpu_custom_call" | custom-call | tf_op jit(solution)/shard_map/pallas_call | solution.py:478

commit v4 on v3

--- a/solution.py
+++ b/solution.py
@@ -16,10 +16,11 @@
 COLS = 8192
 D = 256
 MINE = COLS // NX
-CH = 512
+CH = 256
 NQ = MINE // CH
-HALF = CH // 2
+LAG = 4
 FACTOR = PROTOS / (STUDENT_TEMP * CROPS)
+CROSS = 1.0 / STUDENT_TEMP
 LOG2E = 1.4426950408889634
 MESH = pl.DeviceIdType.MESH
 F32 = jnp.float32
@@ -56,17 +57,15 @@
 
 def kernel(
     te, se, pr, loss, grad,
-    ut, us, ust, up, big, colv, cin, cb, rvec, row_in, az, az_in,
-    land, mine, pz, gb, ring,
-    s_in, s_col, r_col, s_row, r_row, s_x, r_x, s_z, r_z, s_k, r_k, s_az, r_az,
-    s_ring, r_ring, s_out, r_out,
+    ut, us, ust, up, big, colv, cin, cb, rvec, row_in, az, az_in, row_all,
+    land, mine, pz, gb, ring, tot,
+    s_in, s_col, r_col, s_row, r_row, s_x, r_x, s_z, r_z, s_k, r_k, s_az, r_az, s_all, r_all,
+    s_ring, r_ring, s_out, r_out, s_own,
 ):
     mb = lax.axis_index("batch")
     mp = lax.axis_index("proto")
     y, x = mb // NX, lax.rem(mb, NX)
     other = mp + 1 - 2 * lax.rem(mp, 2)
-    gg = big.at[pl.ds(0, D), pl.ds(0, MINE)]
-    wa = [big.at[:, pl.ds(MINE + 128 * d, 128)] for d in range(4)]
     ut0, us0 = gb.at[pl.ds(0, ROWS), pl.ds(0, D)], gb.at[pl.ds(ROWS, ROWS), pl.ds(0, D)]
     wide, part, xp = pz.at[1], pz.at[2], pz.at[3]
 
@@ -78,13 +77,6 @@
 
     def at_z(d):
         return lax.rem(mp + 2 * d, NP)
-
-    barrier = pltpu.get_barrier_semaphore()
-    for d in (1, 2, 3):
-        pl.semaphore_signal(barrier, inc=1, device_id={"batch": at_x(d)}, device_id_type=MESH)
-        pl.semaphore_signal(barrier, inc=1, device_id={"batch": at_y(d)}, device_id_type=MESH)
-    for d in range(1, NP):
-        pl.semaphore_signal(barrier, inc=1, device_id={"proto": lax.rem(mp + d, NP)}, device_id_type=MESH)
 
     fetch = [pltpu.make_async_copy(te, ut0, s_in.at[0]), pltpu.make_async_copy(se, us0, s_in.at[1])]
     for j in range(4):
@@ -92,6 +84,17 @@
         fetch.append(pltpu.make_async_copy(pr.at[:, cols], up.at[:, cols], s_in.at[2 + j]))
     for copy in fetch:
         copy.start()
+    barrier = pltpu.get_barrier_semaphore()
+    for d in (1, 2, 3):
+        pl.semaphore_signal(barrier, inc=1, device_id={"batch": at_y(d)}, device_id_type=MESH)
+
+    def greet(i, carry):
+        there = {"batch": at_x(i // NP), "proto": lax.rem(mp + i, NP)}
+        pl.semaphore_signal(barrier, inc=1, device_id=there, device_id_type=MESH)
+        return carry
+
+    lax.fori_loop(1, NX * NP, greet, 0)
+
     fetch[0].wait()
     ut0[...] = unit(ut0[...], 1)
     fetch[1].wait()
@@ -99,8 +102,6 @@
     slab = pl.ds(pl.multiple_of(mp * 128, 128), 128)
     mine[0, 0] = ut0[slab, :].astype(F32)
     mine[0, 1] = us0[slab, :].astype(F32)
-    pl.semaphore_wait(barrier, 6 + NP - 1)
-
     def x_near(i, p):
         send(mine.at[i], land.at[p, 2], s_x.at[i, 0], r_x.at[i, 0], batch=at_x(1))
         send(mine.at[i], land.at[p, 0], s_x.at[i, 1], r_x.at[i, 1], batch=at_x(3))
@@ -115,13 +116,10 @@
         wait(land.at[p, 1, 0], r_x.at[i, 2])
         wait(land.at[p, 1, 1], r_x.at[i, 3])
 
-    x_near(0, mp)
 
     def col_send(it, ph, k):
-        on_x = lax.rem(k + ph, 2)
-        on_y = 1 - on_x
         for d in (2, 1, 3):
-            to = lax.rem(y + d * on_y, 4) * NX + lax.rem(x + d * on_x, NX)
+            to = at_x(d) if ph else at_y(d)
             send(colv.at[it, ph, k], cin.at[it, ph, k, d - 1], s_col.at[it, ph, k], r_col.at[it, ph, k], batch=to)
 
     def col_recv(it, ph, k):
@@ -144,6 +142,11 @@
         flat = jnp.sum(total, axis=0, keepdims=True)
         for k in range(16):
             colv[0, 0, j, pl.ds(k, 1), :] = flat[:, k * 128 : (k + 1) * 128]
+        @pl.when(j == 0)
+        def _():
+            pl.semaphore_wait(barrier, 3 + NX * NP - 1)
+            x_near(0, mp)
+
         col_send(0, 0, j)
         return carry
 
@@ -195,29 +198,35 @@
         wait(dst.at[pl.ds(0, NP - 1)], r_row.at[k])
         return jnp.sum(dst[...], axis=0)
 
-    def student(r):
-        rows = pl.ds(r * 256, 256)
-        acc = jnp.zeros((256, 128), F32)
-        for j in range(16):
-            s = jnp.dot(us0[rows, :], up[:, pl.ds(j * 512, 512)], preferred_element_type=F32)
-            e = jnp.exp2(s * (LOG2E / STUDENT_TEMP))
-            for k in range(4):
-                acc = acc + e[:, k * 128 : (k + 1) * 128]
-        xp[rows, :] = acc
-
-    def cross(lo, hi):
+    def student(lo, hi):
         def step(r, carry):
             rows = pl.ds(pl.multiple_of(r * 256, 256), 256)
-            v = jnp.zeros((256, D), F32)
-            for g in range(4):
-                cols = pl.ds(g * 2048, 2048)
-                kc = (big[rows, cols] * cb[pl.ds(0, 1), cols]).astype(BF16)
-                v = v + lax.dot_general(kc, up[:, cols], (((1,), (1,)), ((), ())), preferred_element_type=F32)
-            v = v * us0[rows, :].astype(F32)
-            part[rows, :] = v[:, :128] + v[:, 128:]
+            acc = jnp.zeros((256, 128), F32)
+            for j in range(16):
+                s = jnp.dot(us0[rows, :], up[:, pl.ds(j * 512, 512)], preferred_element_type=F32)
+                e = jnp.exp2(s * (LOG2E / STUDENT_TEMP))
+                for k in range(4):
+                    acc = acc + e[:, k * 128 : (k + 1) * 128]
+            xp[rows, :] = acc
             return carry
 
         lax.fori_loop(lo, hi, step, 0)
+
+    def cross(r):
+        rows = pl.ds(pl.multiple_of(r * 256, 256), 256)
+        v = jnp.zeros((256, D), F32)
+        for g in range(4):
+            cols = pl.ds(g * 2048, 2048)
+            kc = (big[rows, cols] * cb[pl.ds(0, 1), cols]).astype(BF16)
+            v = v + lax.dot_general(kc, up[:, cols], (((1,), (1,)), ((), ())), preferred_element_type=F32)
+        v = v * mine_us(r)
+        v = v[:, :128] + v[:, 128:]
+        for i in range(2):
+            rvec[4, pl.ds(2 * r + i, 1), :] = jnp.sum(v[i * 128 : (i + 1) * 128].T, axis=0, keepdims=True)
+
+    def mine_us(r):
+        own = [us[pl.ds(pl.multiple_of((2 * r + i) * 512, 512), 128), :] for i in range(2)]
+        return jnp.concatenate(own, axis=0).astype(F32)
 
     def slabs(p):
         for d in (1, 2, 3):
@@ -230,16 +239,13 @@
 
     z1, z3, z2 = at_z(1), at_z(3), at_z(2)
 
-    col_recv(0, 0, 0)
-    col_send(0, 1, 0)
-    student(0)
-    col_recv(0, 0, 1)
-    col_send(0, 1, 1)
-    col_recv(0, 0, 2)
-    col_send(0, 1, 2)
-    student(1)
-    col_recv(0, 0, 3)
-    col_send(0, 1, 3)
+    for k in range(2):
+        col_recv(0, 0, k)
+        col_send(0, 1, k)
+    student(0, 2)
+    for k in (2, 3):
+        col_recv(0, 0, k)
+        col_send(0, 1, k)
     x_far(0, mp)
     for k in range(4):
         col_recv(0, 1, k)
@@ -257,8 +263,7 @@
     mine[1, 0] = ut0[slab, :].astype(F32)
     mine[1, 1] = us0[slab, :].astype(F32)
     x_near(1, z2)
-    student(2)
-    student(3)
+    student(2, 4)
     rvec[3] = rows_to_vec(xp)
     total = row_recv(rvec.at[0], row_in.at[0], 0)
     vec_to_rows(1.0 / (total * CROPS), wide)
@@ -289,9 +294,9 @@
 
     col_pass(2)
     z = row_recv(rvec.at[3], row_in.at[3], 3)
-    az[0] = FACTOR / z
+    az[...] = FACTOR / z
     for d in (1, 2, 3):
-        send(az.at[0], az_in.at[0, 3 - d], s_az.at[0], r_az.at[0], batch=at_x(d))
+        send(az, az_in.at[0, 3 - d], s_az, r_az, batch=at_x(d))
     for k in range(2):
         wait(land.at[mp, :, 0], r_z.at[0, k])
         wait(land.at[mp, most, 1], r_z.at[1, k])
@@ -302,15 +307,26 @@
     for k in range(4):
         col_recv(2, 0, k)
         col_send(2, 1, k)
-    wait(az_in.at[0], r_az.at[0])
-    vec_to_rows(az[0], pz.at[0])
+    wait(az_in.at[0, pl.ds(0, 3)], r_az)
+    vec_to_rows(az[...], pz.at[0])
     vec_to_rows(az_in[0, 0], pz.at[1])
     vec_to_rows(az_in[0, 2], pz.at[3])
     for k in range(4):
         col_recv(2, 1, k)
         row_pass(2, k)
     rvec[2] = rows_to_vec(part)
-    row_send(rvec.at[2], row_in.at[2], 2)
+
+    def to_all(i, carry):
+        e = i // NP
+        there = lax.rem(mp + i, NP)
+        pltpu.make_async_remote_copy(
+            src_ref=rvec.at[2], dst_ref=row_all.at[lax.rem(NX - e, NX) * NP + mp], send_sem=s_all, recv_sem=r_all,
+            device_id={"batch": at_x(e), "proto": there}, device_id_type=MESH,
+        ).start()
+        return carry
+
+    lax.fori_loop(1, NX * NP, to_all, 0)
+    row_all[mp] = rvec[2]
     slabs(z1)
     slabs(z3)
     slabs(z2)
@@ -318,19 +334,18 @@
         theirs = p + 1 - 2 * lax.rem(p, 2)
         wait(land.at[theirs], r_k.at[k])
         slabs(theirs)
-    cross(0, 2)
-    total = row_recv(rvec.at[2], row_in.at[2], 2)
-    az[1] = FACTOR / total
-    for d in (1, 2, 3):
-        send(az.at[1], az_in.at[1, 3 - d], s_az.at[1], r_az.at[1], batch=at_x(d))
-    cross(2, 4)
-    rvec[4] = rows_to_vec(part) / (total * STUDENT_TEMP)
-    row_send(rvec.at[4], row_in.at[4], 4)
-    vec_to_rows(az[1], wa[0])
     vec_to_rows(az_in[0, 1], pz.at[2])
-    wait(az_in.at[1], r_az.at[1])
-    for g in (1, 2, 3):
-        vec_to_rows(az_in[1, g - 1], wa[g])
+    for k in range(4):
+        wait(land.at[mp], s_k.at[k])
+    for k in range(2):
+        wait(land.at[mp, :, 0], s_z.at[0, k])
+        wait(land.at[mp, most, 1], s_z.at[1, k])
+        wait(land.at[mp, 2, 1], s_z.at[2, k])
+        for i in range(2):
+            wait(mine.at[0, 0], s_x.at[i, 2 + k])
+    wait(row_all.at[pl.ds(0, NX * NP - 1)], r_all)
+    for d in range(NX):
+        az_in[1, d] = FACTOR / jnp.sum(row_all[pl.ds(d * NP, NP)], axis=0)
 
     base = x * MINE
 
@@ -344,42 +359,43 @@
             own = pl.ds(p * 128, 128)
             s = jnp.dot(us[rows, :], w, preferred_element_type=F32)
             t = jnp.dot(ut[rows, :], w, preferred_element_type=F32)
-            a = jnp.concatenate([wa[d][own, :] for d in range(4)], axis=0)
+            a = [jnp.broadcast_to(az_in[1, d, p : p + 1, :], (128, 128)).T for d in range(4)]
+            a = jnp.concatenate(a, axis=0)
             e = jnp.concatenate([pz[d, own, :] for d in range(4)], axis=0)
             t = jnp.exp2(t * (LOG2E / TEACHER_TEMP)) * jnp.concatenate([a] * n, axis=1) * c
             s = jnp.exp2(s * (LOG2E / STUDENT_TEMP)) * jnp.concatenate([e] * n, axis=1)
             gb[rows, :] = (s - t).astype(BF16)
-        gg[:, pl.ds(pl.multiple_of(q * CH, CH), CH)] = jnp.dot(ust[...], gb[...], preferred_element_type=F32)
-
-    def lanes_of(q, h):
-        return pl.ds(pl.multiple_of(q * CH + h * HALF, HALF), HALF)
-
-    def rows_of(d):
-        return pl.ds(pl.multiple_of(lax.rem(y + d, 4) * 64, 64), 64)
+        g = jnp.dot(ust[...], gb[...], preferred_element_type=F32)
+        land[q, 0, 0] = g[:128]
+        land[q, 0, 1] = g[128:]
+
+    def part_of(q, h, d):
+        to = lax.rem(y + d, 4)
+        return land.at[q, 0, to // 2, pl.ds(pl.multiple_of(lax.rem(to, 2) * 64 + h * 32, 32), 32)]
 
     def ring_first(q):
         for h in range(2):
             near, far = (1, 3) if h == 0 else (3, 1)
-            send(gg.at[rows_of(2), lanes_of(q, h)], ring.at[q, h, 0], s_ring.at[q, h, 0], r_ring.at[q, h, 0], batch=at_y(far))
-            send(gg.at[rows_of(near), lanes_of(q, h)], ring.at[q, h, 1], s_ring.at[q, h, 1], r_ring.at[q, h, 1], batch=at_y(near))
+            send(part_of(q, h, 2), ring.at[q, h, 0], s_ring.at[q, h, 0], r_ring.at[q, h, 0], batch=at_y(far))
+            send(part_of(q, h, near), ring.at[q, h, 1], s_ring.at[q, h, 1], r_ring.at[q, h, 1], batch=at_y(near))
 
     def ring_second(q):
         for h in range(2):
             far = 3 if h == 0 else 1
             wait(ring.at[q, h, 0], r_ring.at[q, h, 0])
-            ring[q, h, 0] = ring[q, h, 0] + gg[rows_of(far), lanes_of(q, h)]
+            ring[q, h, 0] = ring[q, h, 0] + part_of(q, h, far)[...]
             send(ring.at[q, h, 0], ring.at[q, h, 2], s_ring.at[q, h, 2], r_ring.at[q, h, 2], batch=at_y(far))
 
     def ring_last(q):
         for h in range(2):
             wait(ring.at[q, h, 1], r_ring.at[q, h, 1])
             wait(ring.at[q, h, 2], r_ring.at[q, h, 2])
-            ring[q, h, 1] = gg[rows_of(0), lanes_of(q, h)] + ring[q, h, 1] + ring[q, h, 2]
-            cols = pl.ds(pl.multiple_of(base + q * CH + h * HALF, HALF), HALF)
-            for d in (2, 1, 3):
-                to = pl.ds(pl.multiple_of(lax.rem(x + d, NX) * 16, 16), 16)
-                send(ring.at[q, h, 1, to], grad.at[:, cols], s_out, r_out, batch=at_x(d))
-            grad[:, cols] = ring[q, h, 1, pl.ds(pl.multiple_of(x * 16, 16), 16)]
+            tot[q, pl.ds(h * 32, 32)] = part_of(q, h, 0)[...] + ring[q, h, 1] + ring[q, h, 2]
+        cols = pl.ds(pl.multiple_of(base + q * CH, CH), CH)
+        for d in (2, 1, 3):
+            to = pl.ds(pl.multiple_of(lax.rem(x + d, NX) * 16, 16), 16)
+            send(tot.at[q, to], grad.at[:, cols], s_out, r_out, batch=at_x(d))
+        pltpu.make_async_copy(tot.at[q, pl.ds(pl.multiple_of(x * 16, 16), 16)], grad.at[:, cols], s_own).start()
 
     def last(q, carry):
         @pl.when(q < NQ)
@@ -387,39 +403,42 @@
             block(q)
             ring_first(q)
 
-        @pl.when((q >= 1) & (q <= NQ))
+        @pl.when((q >= LAG) & (q < NQ + LAG))
         def _():
-            ring_second(q - 1)
-
-        @pl.when(q >= 2)
+            ring_second(q - LAG)
+
+        @pl.when(q >= 2 * LAG)
         def _():
-            ring_last(q - 2)
+            ring_last(q - 2 * LAG)
+
+        @pl.when((q >= NQ) & (q < NQ + 4))
+        def _():
+            cross(q - NQ)
+
+        @pl.when(q == NQ + 3)
+        def _():
+            rvec[4] = rvec[4] * CROSS / jnp.sum(row_all[pl.ds(0, NP)], axis=0)
+            row_send(rvec.at[4], row_in.at[4], 4)
 
         return carry
 
-    lax.fori_loop(0, NQ + 2, last, 0)
+    lax.fori_loop(0, NQ + 2 * LAG, last, 0)
     loss[...] = jnp.log(z) - row_recv(rvec.at[4], row_in.at[4], 4)
 
     wait(grad.at[:, pl.ds(0, 3 * MINE)], r_out)
     wait(grad.at[:, pl.ds(0, 3 * MINE)], s_out)
+    wait(grad.at[:, pl.ds(0, MINE)], s_own)
     for it in range(ITERS):
         for ph in range(2):
             for k in range(4):
                 wait(cin.at[it, ph, k], s_col.at[it, ph, k])
-    for k in range(5):
+    for k in (0, 1, 3, 4):
         wait(row_in.at[k, pl.ds(0, NP - 1)], s_row.at[k])
     for i in range(2):
         for k in range(2):
             wait(mine.at[0], s_x.at[i, k])
-            wait(mine.at[0, 0], s_x.at[i, 2 + k])
-    for k in range(2):
-        wait(land.at[mp, :, 0], s_z.at[0, k])
-        wait(land.at[mp, most, 1], s_z.at[1, k])
-        wait(land.at[mp, 2, 1], s_z.at[2, k])
-    for k in range(4):
-        wait(land.at[mp], s_k.at[k])
-    for k in range(2):
-        wait(az_in.at[k], s_az.at[k])
+    wait(az_in.at[0, pl.ds(0, 3)], s_az)
+    wait(row_all.at[pl.ds(0, NX * NP - 1)], s_all)
     for q in range(NQ):
         for h in range(2):
             for k in range(3):
@@ -442,7 +461,7 @@
             jax.ShapeDtypeStruct((16, COLS), F32),
         ),
         in_specs=[hbm] * 3,
-        out_specs=(vmem, vmem),
+        out_specs=(vmem, hbm),
         scratch_shapes=[
             pltpu.VMEM((NX * ROWS, D), BF16),
             pltpu.VMEM((NX * ROWS, D), BF16),
@@ -454,22 +473,25 @@
             pltpu.VMEM((8, COLS), F32),
             pltpu.VMEM((5, 8, 128), F32),
             pltpu.VMEM((5, NP, 8, 128), F32),
-            pltpu.VMEM((2, 8, 128), F32),
-            pltpu.VMEM((2, 3, 8, 128), F32),
+            pltpu.VMEM((8, 128), F32),
+            pltpu.VMEM((2, NX, 8, 128), F32),
+            pltpu.VMEM((NX * NP, 8, 128), F32),
             pltpu.VMEM((NP, 3, 2, 128, D), F32),
             pltpu.VMEM((2, 2, 128, D), F32),
             pltpu.VMEM((NX, ROWS, 128), F32),
             pltpu.VMEM((NX * ROWS, CH), BF16),
-            pltpu.VMEM((NQ, 2, 3, 64, HALF), F32),
+            pltpu.VMEM((NQ, 2, 3, 32, CH), F32),
+            pltpu.VMEM((NQ, 64, CH), F32),
             dma((6,)),
             dma((ITERS, 2, 4)), dma((ITERS, 2, 4)),
             dma((5,)), dma((5,)),
             dma((2, 4)), dma((2, 4)),
             dma((3, 2)), dma((3, 2)),
             dma((4,)), dma((4,)),
-            dma((2,)), dma((2,)),
+            dma, dma,
+            dma, dma,
             dma((NQ, 2, 3)), dma((NQ, 2, 3)),
-            dma, dma,
+            dma, dma, dma,
         ],
         compiler_params=pltpu.CompilerParams(
             collective_id=0, has_side_effects=True, vmem_limit_bytes=63 * 1024 * 1024

time: 94.4 us -> 90.5 us (0.959)
  Pallas kernels: 93.3 us -> 89.7 us
    pallas_call x1, Pallas kernels: 91.4 us -> 87.8 us  [local(): pl.pallas_call(kernel, out_shape=(jax.ShapeDtypeStruct((8, 128), F32), ja...]
where the time goes in v4:
time: 90.5 us; the launch traced here: 90.4 us
  Pallas kernels  89.7 us (99%)
    pallas_call x1, Pallas kernels, local(): pl.pallas_call(kernel, out_shape=(jax.ShapeDtypeStruct((8, 128), F32), ja...  87.8 us
    pallas_call x1, Pallas kernels, local(): pl.pallas_call(handover, out_shape=(jax.ShapeDtypeStruct((8, 128), F32),...  1.88 us

profile of v4, /device:TPU:0, one launch (start us, length us, event | category | flops | bytes accessed | tf_op | source)
XLA Modules:
  0.0 90.4 jit_solution(1624517652727987734)
XLA Ops:
  0.6 87.8 %shard_map.50 = (f32[8,128]{1,0:T(8,128)}, f32[16,8192]{1,0:T(8,128)}) custom-call(bf16[1024,256]{1,0:T(8,128)(2,1)} %te.1, bf16[1024,256]{1,0:T(8,128)(2,1)} %se.1, bf16[256,8192]{1,0:T(8,128)(2,1)} %pr.1), custom_call_target="tpu_custom_call" | custom-call | tf_op jit(solution)/shard_map/pallas_call | solution.py:457
  88.5 1.9 %shard_map.51 = (f32[8,128]{1,0:T(8,128)}, f32[16,8192]{1,0:T(8,128)}) custom-call(f32[8,128]{1,0:T(8,128)} %get-tuple-element.6.loss, f32[16,8192]{1,0:T(8,128)} %get-tuple-element.7.grad), custom_call_target="tpu_custom_call" | custom-call | tf_op jit(solution)/shard_map/pallas_call | solution.py:500

commit v5 on v4

--- a/solution.py
+++ b/solution.py
@@ -120,7 +120,7 @@
     def col_send(it, ph, k):
         for d in (2, 1, 3):
             to = at_x(d) if ph else at_y(d)
-            send(colv.at[it, ph, k], cin.at[it, ph, k, d - 1], s_col.at[it, ph, k], r_col.at[it, ph, k], batch=to)
+            send(colv.at[it, ph, k], cin.at[it, ph, k, d - 1], s_col, r_col.at[it, ph, k], batch=to)
 
     def col_recv(it, ph, k):
         wait(cin.at[it, ph, k], r_col.at[it, ph, k])
@@ -335,6 +335,12 @@
         wait(land.at[theirs], r_k.at[k])
         slabs(theirs)
     vec_to_rows(az_in[0, 1], pz.at[2])
+
+    def early(r, carry):
+        cross(r)
+        return carry
+
+    lax.fori_loop(0, 2, early, 0)
     for k in range(4):
         wait(land.at[mp], s_k.at[k])
     for k in range(2):
@@ -376,15 +382,15 @@
     def ring_first(q):
         for h in range(2):
             near, far = (1, 3) if h == 0 else (3, 1)
-            send(part_of(q, h, 2), ring.at[q, h, 0], s_ring.at[q, h, 0], r_ring.at[q, h, 0], batch=at_y(far))
-            send(part_of(q, h, near), ring.at[q, h, 1], s_ring.at[q, h, 1], r_ring.at[q, h, 1], batch=at_y(near))
+            send(part_of(q, h, 2), ring.at[q, h, 0], s_ring, r_ring.at[q, h, 0], batch=at_y(far))
+            send(part_of(q, h, near), ring.at[q, h, 1], s_ring, r_ring.at[q, h, 1], batch=at_y(near))
 
     def ring_second(q):
         for h in range(2):
             far = 3 if h == 0 else 1
             wait(ring.at[q, h, 0], r_ring.at[q, h, 0])
             ring[q, h, 0] = ring[q, h, 0] + part_of(q, h, far)[...]
-            send(ring.at[q, h, 0], ring.at[q, h, 2], s_ring.at[q, h, 2], r_ring.at[q, h, 2], batch=at_y(far))
+            send(ring.at[q, h, 0], ring.at[q, h, 2], s_ring, r_ring.at[q, h, 2], batch=at_y(far))
 
     def ring_last(q):
         for h in range(2):
@@ -411,11 +417,11 @@
         def _():
             ring_last(q - 2 * LAG)
 
-        @pl.when((q >= NQ) & (q < NQ + 4))
+        @pl.when((q >= NQ) & (q < NQ + 2))
         def _():
-            cross(q - NQ)
-
-        @pl.when(q == NQ + 3)
+            cross(q - NQ + 2)
+
+        @pl.when(q == NQ + 1)
         def _():
             rvec[4] = rvec[4] * CROSS / jnp.sum(row_all[pl.ds(0, NP)], axis=0)
             row_send(rvec.at[4], row_in.at[4], 4)
@@ -428,10 +434,7 @@
     wait(grad.at[:, pl.ds(0, 3 * MINE)], r_out)
     wait(grad.at[:, pl.ds(0, 3 * MINE)], s_out)
     wait(grad.at[:, pl.ds(0, MINE)], s_own)
-    for it in range(ITERS):
-        for ph in range(2):
-            for k in range(4):
-                wait(cin.at[it, ph, k], s_col.at[it, ph, k])
+    wait(cin, s_col)
     for k in (0, 1, 3, 4):
         wait(row_in.at[k, pl.ds(0, NP - 1)], s_row.at[k])
     for i in range(2):
@@ -439,10 +442,7 @@
             wait(mine.at[0], s_x.at[i, k])
     wait(az_in.at[0, pl.ds(0, 3)], s_az)
     wait(row_all.at[pl.ds(0, NX * NP - 1)], s_all)
-    for q in range(NQ):
-        for h in range(2):
-            for k in range(3):
-                wait(ring.at[q, h, k], s_ring.at[q, h, k])
+    wait(ring, s_ring)
 
 
 def handover(loss, grad, loss_out, grad_out):
@@ -483,14 +483,14 @@
             pltpu.VMEM((NQ, 2, 3, 32, CH), F32),
             pltpu.VMEM((NQ, 64, CH), F32),
             dma((6,)),
-            dma((ITERS, 2, 4)), dma((ITERS, 2, 4)),
+            dma, dma((ITERS, 2, 4)),
             dma((5,)), dma((5,)),
             dma((2, 4)), dma((2, 4)),
             dma((3, 2)), dma((3, 2)),
             dma((4,)), dma((4,)),
             dma, dma,
             dma, dma,
-            dma((NQ, 2, 3)), dma((NQ, 2, 3)),
+            dma, dma((NQ, 2, 3)),
             dma, dma, dma,
         ],
         compiler_params=pltpu.CompilerParams(

time: 90.5 us -> 89.4 us (0.988)
  Pallas kernels: 89.7 us -> 88.3 us
    pallas_call x1, Pallas kernels: 87.8 us -> 86.5 us  [local(): pl.pallas_call(kernel, out_shape=(jax.ShapeDtypeStruct((8, 128), F32), ja...]
where the time goes in v5:
time: 89.4 us; the launch traced here: 89 us
  Pallas kernels  88.3 us (99%)
    pallas_call x1, Pallas kernels, local(): pl.pallas_call(kernel, out_shape=(jax.ShapeDtypeStruct((8, 128), F32), ja...  86.5 us
    pallas_call x1, Pallas kernels, local(): pl.pallas_call(handover, out_shape=(jax.ShapeDtypeStruct((8, 128), F32),...  1.88 us

profile of v5, /device:TPU:0, one launch (start us, length us, event | category | flops | bytes accessed | tf_op | source)
XLA Modules:
  0.0 89.0 jit_solution(12465256012247279837)
XLA Ops:
  0.6 86.5 %shard_map.50 = (f32[8,128]{1,0:T(8,128)}, f32[16,8192]{1,0:T(8,128)}) custom-call(bf16[1024,256]{1,0:T(8,128)(2,1)} %te.1, bf16[1024,256]{1,0:T(8,128)(2,1)} %se.1, bf16[256,8192]{1,0:T(8,128)(2,1)} %pr.1), custom_call_target="tpu_custom_call" | custom-call | tf_op jit(solution)/shard_map/pallas_call | solution.py:457
  87.1 1.9 %shard_map.51 = (f32[8,128]{1,0:T(8,128)}, f32[16,8192]{1,0:T(8,128)}) custom-call(f32[8,128]{1,0:T(8,128)} %get-tuple-element.6.loss, f32[16,8192]{1,0:T(8,128)} %get-tuple-element.7.grad), custom_call_target="tpu_custom_call" | custom-call | tf_op jit(solution)/shard_map/pallas_call | solution.py:500

commit v6 on v5

--- a/solution.py
+++ b/solution.py
@@ -18,7 +18,7 @@
 MINE = COLS // NX
 CH = 256
 NQ = MINE // CH
-LAG = 4
+LAG = 3
 FACTOR = PROTOS / (STUDENT_TEMP * CROPS)
 CROSS = 1.0 / STUDENT_TEMP
 LOG2E = 1.4426950408889634
@@ -413,9 +413,9 @@
         def _():
             ring_second(q - LAG)
 
-        @pl.when(q >= 2 * LAG)
+        @pl.when(q >= LAG + 4)
         def _():
-            ring_last(q - 2 * LAG)
+            ring_last(q - LAG - 4)
 
         @pl.when((q >= NQ) & (q < NQ + 2))
         def _():
@@ -428,7 +428,7 @@
 
         return carry
 
-    lax.fori_loop(0, NQ + 2 * LAG, last, 0)
+    lax.fori_loop(0, NQ + LAG + 4, last, 0)
     loss[...] = jnp.log(z) - row_recv(rvec.at[4], row_in.at[4], 4)
 
     wait(grad.at[:, pl.ds(0, 3 * MINE)], r_out)
@@ -445,9 +445,22 @@
     wait(ring, s_ring)
 
 
-def handover(loss, grad, loss_out, grad_out):
-    loss_out[...] = loss[...]
-    grad_out[...] = grad[...]
+def handover(loss, grad, loss_out, grad_out, small, large, sems):
+    def pieces(k):
+        cols = pl.ds(k * 2048, 2048)
+        return grad.at[:, cols], large.at[k], grad_out.at[:, cols]
+
+    into = [pltpu.make_async_copy(pieces(k)[0], large.at[k], sems.at[0, k]) for k in range(4)]
+    into.append(pltpu.make_async_copy(loss, small, sems.at[0, 4]))
+    out = [pltpu.make_async_copy(large.at[k], pieces(k)[2], sems.at[1, k]) for k in range(4)]
+    out.append(pltpu.make_async_copy(small, loss_out, sems.at[1, 4]))
+    for copy in into:
+        copy.start()
+    for k in range(5):
+        into[k].wait()
+        out[k].start()
+    for copy in out:
+        copy.wait()
 
 
 def local(teacher_emb, student_emb, prototypes):
@@ -503,8 +516,9 @@
             jax.ShapeDtypeStruct((8, 128), F32),
             jax.ShapeDtypeStruct((16, COLS), F32),
         ),
-        in_specs=[vmem] * 2,
-        out_specs=(vmem, vmem),
+        in_specs=[hbm] * 2,
+        out_specs=(hbm, hbm),
+        scratch_shapes=[pltpu.VMEM((8, 128), F32), pltpu.VMEM((4, 16, 2048), F32), dma((2, 5))],
     )(loss, grad)
     return loss.reshape(ROWS), grad
 

time: 89.4 us -> 89.2 us (level)
  no operation moved by 1% of the time
where the time goes in v6:
time: 89.2 us; the launch traced here: 89.1 us
  Pallas kernels  88.3 us (99%)
    pallas_call x1, Pallas kernels, local(): pl.pallas_call(kernel, out_shape=(jax.ShapeDtypeStruct((8, 128), F32), ja...  86.5 us
    pallas_call x1, Pallas kernels, local(): pl.pallas_call(handover, out_shape=(jax.ShapeDtypeStruct((8, 128), F32),...  1.84 us

profile of v6, /device:TPU:0, one launch (start us, length us, event | category | flops | bytes accessed | tf_op | source)
XLA Modules:
  0.0 89.1 jit_solution(17224700688497111611)
XLA Ops:
  0.6 86.5 %shard_map.50 = (f32[8,128]{1,0:T(8,128)}, f32[16,8192]{1,0:T(8,128)}) custom-call(bf16[1024,256]{1,0:T(8,128)(2,1)} %te.1, bf16[1024,256]{1,0:T(8,128)(2,1)} %se.1, bf16[256,8192]{1,0:T(8,128)(2,1)} %pr.1), custom_call_target="tpu_custom_call" | custom-call | tf_op jit(solution)/shard_map/pallas_call | solution.py:470
  87.1 1.8 %shard_map.51 = (f32[8,128]{1,0:T(8,128)}, f32[16,8192]{1,0:T(8,128)}) custom-call(f32[8,128]{1,0:T(8,128)} %get-tuple-element.6.loss, f32[16,8192]{1,0:T(8,128)} %get-tuple-element.7.grad), custom_call_target="tpu_custom_call" | custom-call | tf_op jit(solution)/shard_map/pallas_call | solution.py:513
